TPU v7x, 256 devices: a whole 4x4x8 slice. The times are simulated.
256 devices in a mesh: wide: 32 (over z, x), narrow: 8 (over y, core).
Axes of the slice: x: 4, y: 4, z: 8, core: 2. Of those that a mesh axis runs over, the one named last changes fastest.
Arguments:
- feats: bfloat16 [256, 262144], P('narrow', 'wide'), may hold values from -6 to 6
- hilbert_pos: int32 [262144], P('wide'), may hold values from 0 to 262143, as said below
- ln_attn: float32 [256], replicated, may hold values from 0.25 to 1.75
- w_qkv: bfloat16 [3, 256, 256], P(None, None, 'narrow'), may hold values from -3.375 to 3.375
- w_proj: bfloat16 [256, 256], P('narrow'), may hold values from -0.375 to 0.375
- ln_pool: float32 [256], replicated, may hold values from 0.25 to 1.75
- w_pool: bfloat16 [256, 512], P(None, 'narrow'), may hold values from -0.375 to 0.375
- cell_of: int32 [262144], P('wide'), may hold values from 0 to 65535, as said below
Outputs:
- block_out: bfloat16 [256, 262144], P('narrow', 'wide')
- coarse: bfloat16 [512, 65536], P('narrow', 'wide')
- unpooled: bfloat16 [512, 262144], P('narrow', 'wide')
Inputs may be any that keep to these rules, and one draw needn't show every extreme that they name: A permutation: the point at z-order position i (on device i // 8192 of wide) moves to Hilbert position hilbert_pos[i], on device hilbert_pos[i] // 8192. Every device receives exactly 8192 points; a device sends at most 512 points to any one device, and exactly 512 to some device. The point at Hilbert position i pools into cell cell_of[i], owned by device cell_of[i] // 2048. Every owner receives exactly 8192 points; a device sends at most 384 points to any one owner, and exactly 384 to some owner. The live cells of an owner are the first 1024 to 2048 of its range, each with one point or more; the last owner has all 2048 live.
All inputs are finite; a program needn't handle non-finite values.
Results may differ from a plain program's by a relative error of at most 0.009.
The roundings to bfloat16 on the way count: a program that leaves them out, or rounds other values in their place, can miss the bound.
Values may be sent and summed in bfloat16 or wider, within the bound.
A program may use at most 128 MiB of HBM per device.

v0:
```python
import jax
import jax.numpy as jnp
import numpy as np
from jax import lax
from jax.experimental import pallas as pl
from jax.experimental.pallas import tpu as pltpu
from jax.sharding import PartitionSpec as P

HD = 16
HEADS = 16
C = 256
C2 = 512
PATCH = 1024
POINTS = 8192
GROUPS = 32
BANDS = 8
CH = C // BANDS
CH2 = C2 // BANDS
LO = 8
TAB = 128
HROWS = 64
PROWS = 48
CELLS = 2048
CHI = CELLS // LO
BF = jnp.bfloat16
F32 = jnp.float32
NT = (((1,), (1,)), ((), ()))
SCORE = float(HD**-0.5 * np.log2(np.e))


def shape(dims, dtype):
    return jax.ShapeDtypeStruct(dims, dtype)


def one_hot(row, first, count):
    numbers = lax.broadcasted_iota(jnp.int32, (count, row.shape[1]), 0)
    return jnp.where(numbers == row - first, 1.0, 0.0).astype(BF)


def spread(values, low):
    wide = values.astype(F32)
    return jnp.concatenate([jnp.where(low == l, wide, 0.0).astype(BF) for l in range(LO)], axis=0)


def gather_low(product, low, channels):
    total = jnp.where(low == 0, product[:channels], 0.0)
    for l in range(1, LO):
        total += jnp.where(low == l, product[l * channels : (l + 1) * channels], 0.0)
    return total


def make_slots(rows, goals, values, row_ref, low_ref, table_ref):
    k = 512
    before = lax.broadcasted_iota(jnp.int32, (k, k), 0) < lax.broadcasted_iota(jnp.int32, (k, k), 1)
    before = jnp.where(before, 1.0, 0.0).astype(BF)
    carry = jnp.zeros((GROUPS, 1), F32)
    table = jnp.zeros((GROUPS * LO, 2 * TAB), F32)
    for j in range(POINTS // k):
        at = slice(j * k % PATCH, j * k % PATCH + k)
        of = slice(j * k // PATCH, j * k // PATCH + 1)
        goal = goals[of, at]
        member = lax.broadcasted_iota(jnp.int32, (GROUPS, k), 0) == goal
        hot = jnp.where(member, 1.0, 0.0)
        running = jnp.dot(hot.astype(BF), before, preferred_element_type=F32) + carry
        carry = carry + jnp.sum(hot, axis=1, keepdims=True)
        rank = jnp.sum(hot * running, axis=0, keepdims=True).astype(jnp.int32)
        low = jnp.zeros_like(rank)
        for l in range(1, LO):
            low += jnp.where(rank >= l * rows, 1, 0)
        high = rank - low * rows
        row_ref[of, at] = goal * rows + high
        low_ref[of, at] = low
        value = values[of, at] + 1
        which = lax.broadcasted_iota(jnp.int32, (TAB, k), 0) == high
        parts = [
            jnp.where(which, part.astype(F32), 0.0) for part in (value >> 7, value & 127)
        ]
        marks = jnp.concatenate(parts, axis=0).astype(BF)
        table += lax.dot_general(
            one_hot(goal * LO + low, 0, GROUPS * LO), marks, NT, preferred_element_type=F32
        )
    table = (table[:, :TAB] * 128.0 + table[:, TAB:]).astype(jnp.int32) - 1
    table_ref[...] = table.reshape(GROUPS, LO, TAB)


def place(row_ref, spread_ref, first, count):
    total = jnp.zeros((count, spread_ref.shape[0]), F32)
    for j in range(BANDS):
        total += lax.dot_general(
            one_hot(row_ref[j : j + 1, :], first, count),
            spread_ref[:, j * PATCH : (j + 1) * PATCH],
            NT,
            preferred_element_type=F32,
        )
    return total


def normalise(wide, gain_ref):
    average = jnp.mean(wide, axis=0, keepdims=True)
    centred = wide - average
    spread_of = jnp.mean(centred * centred, axis=0, keepdims=True)
    return (centred * lax.rsqrt(spread_of + 1e-05) * gain_ref[...]).astype(BF)


def remote(src, dst, send_sem, recv_sem, wide, narrow):
    return pltpu.make_async_remote_copy(
        src_ref=src,
        dst_ref=dst,
        send_sem=send_sem,
        recv_sem=recv_sem,
        device_id={"wide": wide, "narrow": narrow},
        device_id_type=pl.DeviceIdType.MESH,
    )


class Wide:
    def __init__(self, src, dst, send_sem, recv_sem, sign):
        self.src, self.dst, self.send_sem, self.recv_sem, self.sign = src, dst, send_sem, recv_sem, sign

    def copy(self, t):
        goal = (lax.axis_index("wide") + self.sign * t + GROUPS) % GROUPS
        return remote(
            self.src.at[t],
            self.dst.at[t],
            self.send_sem.at[t],
            self.recv_sem.at[t],
            goal,
            lax.axis_index("narrow"),
        )

    def start(self, group):
        @pl.when(group == 0)
        def _():
            self.dst[0] = self.src[0]

        def one(i, _):
            t = group * 8 + i

            @pl.when(t > 0)
            def _():
                self.copy(t).start()

            return 0

        lax.fori_loop(0, 8, one, 0)

    def wait(self, group):
        def one(i, _):
            t = group * 8 + i

            @pl.when(t > 0)
            def _():
                self.copy(t).wait_recv()

            return 0

        lax.fori_loop(0, 8, one, 0)

    def finish(self):
        lax.fori_loop(1, GROUPS, lambda t, _: self.copy(t).wait_send() or 0, 0)


class Narrow:
    def __init__(self, src, dst, send_sem, recv_sem, whole=False):
        self.src, self.dst, self.send_sem, self.recv_sem = src, dst, send_sem, recv_sem
        self.whole = whole

    def copy(self, step):
        me = lax.axis_index("narrow")
        goal = (me + step) % BANDS
        return remote(
            self.src if self.whole else self.src.at[goal],
            self.dst.at[me],
            self.send_sem.at[step],
            self.recv_sem.at[step],
            lax.axis_index("wide"),
            goal,
        )

    def start(self):
        me = lax.axis_index("narrow")
        lax.fori_loop(1, BANDS, lambda s, _: self.copy(s).start() or 0, 0)
        self.dst[me] = self.src[...] if self.whole else self.src[me]

    def wait(self):
        me = lax.axis_index("narrow")

        def one(step, _):
            landed = self.dst.at[(me - step + BANDS) % BANDS]
            remote(
                landed,
                landed,
                self.send_sem.at[step],
                self.recv_sem.at[step],
                lax.axis_index("wide"),
                me,
            ).wait_recv()
            return 0

        lax.fori_loop(1, BANDS, one, 0)

    def finish(self):
        lax.fori_loop(1, BANDS, lambda s, _: self.copy(s).wait_send() or 0, 0)


def attend(x_ref, q_ref, k_ref, v_ref, km_ref, vm_ref, att_ref):
    att_ref[...] = jnp.zeros_like(att_ref)
    rows = 256

    def one_head(h, _):
        dims = lax.broadcasted_iota(jnp.int32, (C, PATCH), 0) // HD
        km_ref[...] = jnp.where(dims == h, k_ref[...].astype(F32), 0.0).astype(BF)
        lanes = lax.broadcasted_iota(jnp.int32, (PATCH, C), 1) // HD
        vm_ref[...] = jnp.where(lanes == h, v_ref[...].astype(F32), 1.0).astype(BF)
        lane = lax.broadcasted_iota(jnp.int32, (rows, C), 1)
        other = lax.rem(h * HD + C // 2, C)
        for b in range(PATCH // rows):
            at = slice(b * rows, (b + 1) * rows)
            scores = jnp.dot(q_ref[at, :], km_ref[...], preferred_element_type=F32)
            top = jnp.max(scores, axis=1, keepdims=True)
            expo = jnp.exp2((scores - top) * SCORE).astype(BF)
            sums = jnp.dot(expo, vm_ref[...], preferred_element_type=F32)
            whole = jnp.sum(jnp.where(lane == other, sums, 0.0), axis=1, keepdims=True)
            att_ref[at, :] += jnp.where(lane // HD == h, sums * (1.0 / whole), 0.0)
        return 0

    lax.fori_loop(0, HEADS, one_head, 0)


def lanes_of(table_ref, group, rows):
    return jnp.concatenate([table_ref[group * 8 + i, :, :rows] for i in range(8)], axis=1)


def kernel(
    feats_ref, hilbert_ref, cell_ref, own_ref, gain_ref, gain2_ref,
    block_ref, coarse_ref, unpooled_ref,
    row_ref, low_ref, p_row_ref, p_low_ref,
    land_out, land_in, cell_out, cell_in,
    spread_ref, first_out, first_in, acc_ref,
    patch_out, patch_in, weights_ref,
    x_ref, q_ref, k_ref, v_ref, km_ref, vm_ref, att_ref,
    both_out, both_in, second_out, second_in,
    sum_ref, count_ref, mean_out, mean_in, table_out, table_in,
    turned_ref, back_out, back_in,
    wide_send, wide_recv, narrow_send, narrow_recv,
):
    me = lax.axis_index("wide")
    mine = lax.axis_index("narrow")

    def wide(number, src, dst, sign=1):
        return Wide(src, dst, wide_send.at[number], wide_recv.at[number], sign)

    def narrow(number, src, dst, whole=False):
        return Narrow(src, dst, narrow_send.at[number], narrow_recv.at[number], whole)

    landings = wide(0, land_out, land_in)
    first = wide(1, first_out, first_in)
    cells = wide(2, cell_out, cell_in)
    second = wide(3, second_out, second_in)
    back = wide(4, back_out, back_in, -1)
    gather = narrow(0, own_ref, weights_ref, True)
    patches = narrow(1, patch_out, patch_in)
    boths = narrow(2, both_out, both_in)
    means = narrow(3, mean_out, mean_in)
    tables = narrow(4, table_out, table_in)

    barrier = pltpu.get_barrier_semaphore()

    def greet_wide(t, _):
        pl.semaphore_signal(
            barrier,
            inc=1,
            device_id={"wide": (me + t) % GROUPS, "narrow": mine},
            device_id_type=pl.DeviceIdType.MESH,
        )
        return 0

    def greet_narrow(t, _):
        pl.semaphore_signal(
            barrier,
            inc=1,
            device_id={"wide": me, "narrow": (mine + t) % BANDS},
            device_id_type=pl.DeviceIdType.MESH,
        )
        return 0

    lax.fori_loop(1, GROUPS, greet_wide, 0)
    lax.fori_loop(1, BANDS, greet_narrow, 0)

    position = hilbert_ref[...]
    make_slots(
        HROWS, ((position >> 13) - me) & (GROUPS - 1), position & (POINTS - 1), row_ref, low_ref, land_out
    )
    for j in range(BANDS):
        at = slice(j * PATCH, (j + 1) * PATCH)
        spread_ref[:, at] = spread(feats_ref[:, at], low_ref[j : j + 1, :])
    pl.semaphore_wait(barrier, GROUPS + BANDS - 2)
    gather.start()
    for g in range(4):
        landings.start(g)

    def first_block(g, _):
        chunk = place(row_ref, spread_ref, g * 512, 512).astype(BF)
        first_out[pl.ds(g * 8, 8)] = chunk.reshape(8, HROWS, LO * CH)
        first.start(g)
        return 0

    lax.fori_loop(0, 4, first_block, 0)

    cell = cell_ref[...]
    make_slots(
        PROWS, ((cell >> 11) - me) & (GROUPS - 1), cell & (CELLS - 1), p_row_ref, p_low_ref, cell_out
    )
    for g in range(4):
        cells.start(g)

    def first_group(g, _):
        landings.wait(g)
        first.wait(g)
        k = 8 * HROWS
        turned = first_in[pl.ds(g * 8, 8)].reshape(k, LO * CH).T
        landing = lanes_of(land_in, g, HROWS)
        for l in range(LO):
            spread_ref[:, l * k : (l + 1) * k] = spread(
                turned[l * CH : (l + 1) * CH], (landing[l : l + 1] >> 7) & 7
            )
        rows = (landing >> 10) * 128 + (landing & 127)
        for m in range(2):
            total = jnp.zeros((512, LO * CH), F32)
            for l in range(LO):
                total += lax.dot_general(
                    one_hot(rows[l : l + 1], m * 512, 512),
                    spread_ref[:, l * k : (l + 1) * k],
                    NT,
                    preferred_element_type=F32,
                )
            at = slice(m * 512, (m + 1) * 512)
            acc_ref[at, :] = jnp.where(g == 0, total, total + acc_ref[at, :])
        return 0

    lax.fori_loop(0, 4, first_group, 0)
    patch_out[...] = acc_ref[...].astype(BF).reshape(BANDS, PATCH // LO, LO * CH)
    patches.start()
    gather.wait()
    patches.wait()

    for n in range(BANDS):
        turned = patch_in[n].T
        for l in range(LO):
            x_ref[n * CH : (n + 1) * CH, l * 128 : (l + 1) * 128] = turned[l * CH : (l + 1) * CH]
    normed = normalise(x_ref[...].astype(F32), gain_ref)

    def weight(start):
        return jnp.concatenate([weights_ref[n, start : start + CH, :] for n in range(BANDS)], axis=0)

    def project(t):
        return jnp.dot(weight(t * CH), normed, preferred_element_type=F32).astype(BF)

    q_ref[...] = project(0).T
    k_ref[...] = project(1)
    v_ref[...] = project(2).T
    attend(x_ref, q_ref, k_ref, v_ref, km_ref, vm_ref, att_ref)
    added = lax.dot_general(
        weight(3 * CH).T, att_ref[...].astype(BF), NT, preferred_element_type=F32
    )
    block = (x_ref[...].astype(F32) + added).astype(BF)
    pooled = normalise(block.astype(F32), gain2_ref)
    for n in range(BANDS):
        both_out[n, :CH, :] = pooled[n * CH : (n + 1) * CH]
        both_out[n, CH:, :] = block[n * CH : (n + 1) * CH]
    boths.start()
    boths.wait()

    for j in range(BANDS):
        at = slice(j * PATCH, (j + 1) * PATCH)
        spread_ref[:, at] = spread(both_in[j, :CH, :], p_low_ref[j : j + 1, :])

    def second_block(g, _):
        chunk = place(p_row_ref, spread_ref, g * 384, 384).astype(BF)
        second_out[pl.ds(g * 8, 8)] = chunk.reshape(8, PROWS, LO * CH)
        second.start(g)
        return 0

    lax.fori_loop(0, 4, second_block, 0)
    for j in range(BANDS):
        block_ref[:, j * PATCH : (j + 1) * PATCH] = both_in[j, CH:, :]
    sum_ref[...] = jnp.zeros_like(sum_ref)
    count_ref[...] = jnp.zeros_like(count_ref)
    k = 8 * PROWS

    def count_group(g, _):
        cells.wait(g)
        cell = lanes_of(cell_in, g, PROWS)
        ones = jnp.ones((CH, k), F32)
        for l in range(LO):
            count_ref[...] += lax.dot_general(
                one_hot(cell[l : l + 1] & (CHI - 1), 0, CHI),
                spread(ones, cell[l : l + 1] >> 8),
                NT,
                preferred_element_type=F32,
            )
        return 0

    lax.fori_loop(0, 4, count_group, 0)

    def second_group(g, _):
        second.wait(g)
        turned = second_in[pl.ds(g * 8, 8)].reshape(k, LO * CH).T
        cell = lanes_of(cell_in, g, PROWS)
        for l in range(LO):
            sum_ref[...] += lax.dot_general(
                one_hot(cell[l : l + 1] & (CHI - 1), 0, CHI),
                spread(turned[l * CH : (l + 1) * CH], cell[l : l + 1] >> 8),
                NT,
                preferred_element_type=F32,
            )
        return 0

    lax.fori_loop(0, 4, second_group, 0)
    mean_out[...] = (sum_ref[...] / jnp.maximum(count_ref[...], 1.0)).T.reshape(BANDS, CH, CHI)
    means.start()
    means.wait()

    mean = mean_in[...].reshape(C, CHI)
    upper = mean.astype(BF)
    lower = (mean - upper.astype(F32)).astype(BF)
    for n in range(BANDS):
        weight_n = weights_ref[n, 4 * CH :, :]
        value = jnp.dot(weight_n, upper, preferred_element_type=F32) + jnp.dot(
            weight_n, lower, preferred_element_type=F32
        )
        table_out[n] = (value * (1.0 + lax.erf(value * (0.5**0.5))) * 0.5).astype(BF)
    tables.start()
    tables.wait()

    table = table_in[...].reshape(BANDS * CH2, CHI)

    def give_group(g, _):
        cell = lanes_of(cell_in, g, PROWS)
        for l in range(LO):
            product = jnp.dot(
                table, one_hot(cell[l : l + 1] & (CHI - 1), 0, CHI), preferred_element_type=F32
            )
            turned_ref[l * CH2 : (l + 1) * CH2, :] = gather_low(
                product, cell[l : l + 1] >> 8, CH2
            ).astype(BF)
        back_out[pl.ds(g * 8, 8)] = turned_ref[...].T.reshape(8, PROWS, LO * CH2)
        back.start(g)
        return 0

    lax.fori_loop(0, 4, give_group, 0)
    for n in range(BANDS):
        coarse_ref[:, n * CHI : (n + 1) * CHI] = table_in[n]
    unpooled_ref[...] = jnp.zeros_like(unpooled_ref)

    def take_group(g, _):
        back.wait(g)
        turned_ref[...] = back_in[pl.ds(g * 8, 8)].reshape(k, LO * CH2).T
        for j in range(BANDS):
            at = slice(j * PATCH, (j + 1) * PATCH)
            product = jnp.dot(
                turned_ref[...], one_hot(p_row_ref[j : j + 1, :], g * k, k), preferred_element_type=F32
            )
            part = gather_low(product, p_low_ref[j : j + 1, :], CH2)
            unpooled_ref[:, at] = (unpooled_ref[:, at].astype(F32) + part).astype(BF)
        return 0

    lax.fori_loop(0, 4, take_group, 0)
    for each in (landings, first, cells, second, back, gather, patches, boths, means, tables):
        each.finish()


def on_device(feats, hilbert_pos, ln_attn, w_qkv, w_proj, ln_pool, w_pool, cell_of):
    own = jnp.concatenate([w_qkv.transpose(0, 2, 1).reshape(-1, C), w_proj, w_pool.T], axis=0)
    small = lambda: pltpu.VMEM((BANDS, PATCH), jnp.int32)
    table = lambda: pltpu.VMEM((GROUPS, LO, TAB), jnp.int32)
    half = lambda *dims: pltpu.VMEM(dims, BF)
    full = lambda *dims: pltpu.VMEM(dims, F32)
    return tuple(
        pl.pallas_call(
            kernel,
            out_shape=[
                jax.ShapeDtypeStruct((CH, POINTS), BF),
                jax.ShapeDtypeStruct((CH2, CELLS), BF),
                jax.ShapeDtypeStruct((CH2, POINTS), BF),
            ],
            in_specs=[pl.BlockSpec(memory_space=pltpu.VMEM)] * 6,
            out_specs=[pl.BlockSpec(memory_space=pltpu.VMEM)] * 3,
            scratch_shapes=[
                small(), small(), small(), small(),
                table(), table(), table(), table(),
                half(LO * CH, POINTS),
                half(GROUPS, HROWS, LO * CH), half(GROUPS, HROWS, LO * CH),
                full(PATCH, LO * CH),
                half(BANDS, PATCH // LO, LO * CH), half(BANDS, PATCH // LO, LO * CH),
                half(BANDS, 6 * CH, C),
                half(C, PATCH), half(PATCH, C), half(C, PATCH), half(PATCH, C),
                half(C, PATCH), half(PATCH, C), full(PATCH, C),
                half(BANDS, 2 * CH, PATCH), half(BANDS, 2 * CH, PATCH),
                half(GROUPS, PROWS, LO * CH), half(GROUPS, PROWS, LO * CH),
                full(CHI, LO * CH), full(CHI, LO * CH),
                full(BANDS, CH, CHI), full(BANDS, CH, CHI),
                half(BANDS, CH2, CHI), half(BANDS, CH2, CHI),
                half(LO * CH2, 8 * PROWS),
                half(GROUPS, PROWS, LO * CH2), half(GROUPS, PROWS, LO * CH2),
                pltpu.SemaphoreType.DMA((5, GROUPS)), pltpu.SemaphoreType.DMA((5, GROUPS)),
                pltpu.SemaphoreType.DMA((5, BANDS)), pltpu.SemaphoreType.DMA((5, BANDS)),
            ],
            compiler_params=pltpu.CompilerParams(
                collective_id=0, has_side_effects=True, vmem_limit_bytes=56 * 1024 * 1024
            ),
        )(
            feats,
            hilbert_pos.reshape(BANDS, PATCH),
            cell_of.reshape(BANDS, PATCH),
            own,
            ln_attn.reshape(C, 1),
            ln_pool.reshape(C, 1),
        )
    )


def solution(mesh):
    in_specs = (
        P("narrow", "wide"),
        P("wide"),
        P(),
        P(None, None, "narrow"),
        P("narrow", None),
        P(),
        P(None, "narrow"),
        P("wide"),
    )
    out_specs = (P("narrow", "wide"), P("narrow", "wide"), P("narrow", "wide"))
    return jax.shard_map(
        on_device, mesh=mesh, in_specs=in_specs, out_specs=out_specs, check_vma=False
    )
```

profile of v0, /device:TPU:96, one launch (start us, length us, event | category | flops | bytes accessed | tf_op | source)
XLA Modules:
  0.0 205.1 jit_solution(7340237050393185554)
XLA Ops:
  0.6 0.0 copy-start.2
  0.6 0.0 copy-start.1
  0.7 1.4 reshape.21.hilbert_ref
  2.0 0.0 copy-done.2
  2.0 0.0 copy-start.3
  2.0 0.0 copy-start.4
  2.0 0.6 reshape.22.cell_ref
  2.7 0.0 copy-done.1
  2.7 0.1 copy-done.3
  2.8 0.0 copy-done.4
  2.8 0.0 copy-start.5
  2.8 0.6 pad_maximum_fusion.own_ref
  3.5 0.0 copy-done.5
  3.5 0.0 copy-start.6
  3.5 0.8 copy.11.gain_ref
  4.3 0.0 copy-done.6
  4.3 0.8 copy.12.gain2_ref
  5.1 195.4 %shard_map.103 = (bf16[32,8192]{1,0:T(8,128)(2,1)}, bf16[64,2048]{1,0:T(8,128)(2,1)}, bf16[64,8192]{1,0:T(8,128)(2,1)}) custom-call(bf16[32,8192]{1,0:T(8,128)(2,1)} %feats_ref.1, s32[8,1024]{1,0:T(8,128)} %reshape.21.hilbert_ref, s32[8,1024]{1,0:T(8,128)} %reshape.22.cell_ref, bf16[192,256]{1,0:T(8,128)(2,1)} %pad_maximum_fusion.own_ref, ...), custom_call_target="tpu_custom_call" | custom-call | tf_op jit(solution)/shard_map/pallas_call | solution.py:480
  200.5 0.0 copy-start
  200.5 2.0 copy.16
  202.5 1.7 copy.17
  204.2 0.0 copy-done
  204.2 1.0 copy.18
Async XLA Ops:
  0.6 1.4 copy-start.2
  0.6 2.0 copy-start.1
  2.0 0.8 copy-start.3
  2.0 0.8 copy-start.4
  2.8 0.7 copy-start.5
  3.5 0.8 copy-start.6
  200.5 3.6 %copy-start = (bf16[64,8192]{1,0:T(8,128)(2,1)S(1)}, bf16[64,8192]{1,0:T(8,128)(2,1)}, u32[]{:S(2)}) copy-start(bf16[64,8192]{1,0:T(8,128)(2,1)} %get-tuple-element.8) | copy-start | bytes 3145732
where the time goes:
time: 205 us
  Pallas kernels  195 us (95%)
  local copies, waits for them, and re-layouts  8.39 us (4%)
    pallas_call x1, Pallas kernels, on_device(): pl.pallas_call(kernel, out_shape=[jax.ShapeDtypeStruct((CH, POINTS), BF),...  195 us
    unnamed x17, local copies, waits for them, and re-layouts  4.79 us

commit v1 on v0

--- a/solution.py
+++ b/solution.py
@@ -18,6 +18,8 @@
 CH2 = C2 // BANDS
 LO = 8
 TAB = 128
+OWN = 1
+COLS = 512
 HROWS = 64
 PROWS = 48
 CELLS = 2048
@@ -49,16 +51,30 @@
     return total
 
 
-def make_slots(rows, goals, values, row_ref, low_ref, table_ref):
+def slot_of(goal):
+    me = lax.axis_index("wide")
+    up = ((goal >> 2) - (me >> 2)) & 7
+    across = ((goal & 3) - (me & 3)) & 3
+    back = jnp.where((up == 0) | (up > 4), 1, 0)
+    return jnp.where(up == 0, 0, jnp.abs(up - 4)) * 8 + across * 2 + back
+
+
+def partner(t, sign):
+    me = lax.axis_index("wide")
+    group, across, back = t // 8, t % 8 // 2, t % 2
+    up = (1 - back) * (4 - group) + back * ((group + 3) // 4 * 4 + group)
+    return (me // 4 + sign * up + 8) % 8 * 4 + (me % 4 + sign * across + 4) % 4
+
+
+def rank_points(rows, bits, goal_ref, row_ref, low_ref):
     k = 512
     before = lax.broadcasted_iota(jnp.int32, (k, k), 0) < lax.broadcasted_iota(jnp.int32, (k, k), 1)
     before = jnp.where(before, 1.0, 0.0).astype(BF)
     carry = jnp.zeros((GROUPS, 1), F32)
-    table = jnp.zeros((GROUPS * LO, 2 * TAB), F32)
     for j in range(POINTS // k):
         at = slice(j * k % PATCH, j * k % PATCH + k)
         of = slice(j * k // PATCH, j * k // PATCH + 1)
-        goal = goals[of, at]
+        goal = slot_of(goal_ref[:, j * k : (j + 1) * k] >> bits)
         member = lax.broadcasted_iota(jnp.int32, (GROUPS, k), 0) == goal
         hot = jnp.where(member, 1.0, 0.0)
         running = jnp.dot(hot.astype(BF), before, preferred_element_type=F32) + carry
@@ -67,17 +83,29 @@
         low = jnp.zeros_like(rank)
         for l in range(1, LO):
             low += jnp.where(rank >= l * rows, 1, 0)
-        high = rank - low * rows
-        row_ref[of, at] = goal * rows + high
+        row_ref[of, at] = goal * rows + rank - low * rows
         low_ref[of, at] = low
-        value = values[of, at] + 1
-        which = lax.broadcasted_iota(jnp.int32, (TAB, k), 0) == high
+
+
+def make_table(rows, bits, value_ref, row_ref, low_ref, table_ref):
+    k = 512
+    table = jnp.zeros((GROUPS * LO, 2 * TAB), F32)
+    for j in range(POINTS // k):
+        at = slice(j * k % PATCH, j * k % PATCH + k)
+        of = slice(j * k // PATCH, j * k // PATCH + 1)
+        values = value_ref[:, j * k : (j + 1) * k]
+        goal = slot_of(values >> bits)
+        value = (values & ((1 << bits) - 1)) + 1
+        which = lax.broadcasted_iota(jnp.int32, (TAB, k), 0) == row_ref[of, at] - goal * rows
         parts = [
             jnp.where(which, part.astype(F32), 0.0) for part in (value >> 7, value & 127)
         ]
         marks = jnp.concatenate(parts, axis=0).astype(BF)
         table += lax.dot_general(
-            one_hot(goal * LO + low, 0, GROUPS * LO), marks, NT, preferred_element_type=F32
+            one_hot(goal * LO + low_ref[of, at], 0, GROUPS * LO),
+            marks,
+            NT,
+            preferred_element_type=F32,
         )
     table = (table[:, :TAB] * 128.0 + table[:, TAB:]).astype(jnp.int32) - 1
     table_ref[...] = table.reshape(GROUPS, LO, TAB)
@@ -95,11 +123,15 @@
     return total
 
 
-def normalise(wide, gain_ref):
+def statistics(wide):
     average = jnp.mean(wide, axis=0, keepdims=True)
     centred = wide - average
     spread_of = jnp.mean(centred * centred, axis=0, keepdims=True)
-    return (centred * lax.rsqrt(spread_of + 1e-05) * gain_ref[...]).astype(BF)
+    return average, lax.rsqrt(spread_of + 1e-05)
+
+
+def normalise(wide, average, scale, gain):
+    return ((wide - average) * scale * gain).astype(BF)
 
 
 def remote(src, dst, send_sem, recv_sem, wide, narrow):
@@ -117,47 +149,39 @@
     def __init__(self, src, dst, send_sem, recv_sem, sign):
         self.src, self.dst, self.send_sem, self.recv_sem, self.sign = src, dst, send_sem, recv_sem, sign
 
-    def copy(self, t):
-        goal = (lax.axis_index("wide") + self.sign * t + GROUPS) % GROUPS
-        return remote(
-            self.src.at[t],
-            self.dst.at[t],
-            self.send_sem.at[t],
-            self.recv_sem.at[t],
-            goal,
-            lax.axis_index("narrow"),
-        )
+    def each(self, first, count, act):
+        def one(i, _):
+            t = first + i
+
+            @pl.when(t != OWN)
+            def _():
+                act(
+                    remote(
+                        self.src.at[t],
+                        self.dst.at[t],
+                        self.send_sem.at[t],
+                        self.recv_sem.at[t],
+                        partner(t, self.sign),
+                        lax.axis_index("narrow"),
+                    )
+                )
+
+            return 0
+
+        lax.fori_loop(0, count, one, 0)
 
     def start(self, group):
-        @pl.when(group == 0)
+        self.each(group * 8, 8, lambda copy: copy.start())
+
+        @pl.when(group == OWN // 8)
         def _():
-            self.dst[0] = self.src[0]
-
-        def one(i, _):
-            t = group * 8 + i
-
-            @pl.when(t > 0)
-            def _():
-                self.copy(t).start()
-
-            return 0
-
-        lax.fori_loop(0, 8, one, 0)
+            self.dst[OWN] = self.src[OWN]
 
     def wait(self, group):
-        def one(i, _):
-            t = group * 8 + i
-
-            @pl.when(t > 0)
-            def _():
-                self.copy(t).wait_recv()
-
-            return 0
-
-        lax.fori_loop(0, 8, one, 0)
+        self.each(group * 8, 8, lambda copy: copy.wait_recv())
 
     def finish(self):
-        lax.fori_loop(1, GROUPS, lambda t, _: self.copy(t).wait_send() or 0, 0)
+        self.each(0, GROUPS, lambda copy: copy.wait_send())
 
 
 class Narrow:
@@ -203,28 +227,41 @@
         lax.fori_loop(1, BANDS, lambda s, _: self.copy(s).wait_send() or 0, 0)
 
 
-def attend(x_ref, q_ref, k_ref, v_ref, km_ref, vm_ref, att_ref):
-    att_ref[...] = jnp.zeros_like(att_ref)
-    rows = 256
-
-    def one_head(h, _):
-        dims = lax.broadcasted_iota(jnp.int32, (C, PATCH), 0) // HD
-        km_ref[...] = jnp.where(dims == h, k_ref[...].astype(F32), 0.0).astype(BF)
-        lanes = lax.broadcasted_iota(jnp.int32, (PATCH, C), 1) // HD
-        vm_ref[...] = jnp.where(lanes == h, v_ref[...].astype(F32), 1.0).astype(BF)
-        lane = lax.broadcasted_iota(jnp.int32, (rows, C), 1)
-        other = lax.rem(h * HD + C // 2, C)
-        for b in range(PATCH // rows):
-            at = slice(b * rows, (b + 1) * rows)
-            scores = jnp.dot(q_ref[at, :], km_ref[...], preferred_element_type=F32)
-            top = jnp.max(scores, axis=1, keepdims=True)
-            expo = jnp.exp2((scores - top) * SCORE).astype(BF)
-            sums = jnp.dot(expo, vm_ref[...], preferred_element_type=F32)
-            whole = jnp.sum(jnp.where(lane == other, sums, 0.0), axis=1, keepdims=True)
-            att_ref[at, :] += jnp.where(lane // HD == h, sums * (1.0 / whole), 0.0)
-        return 0
-
-    lax.fori_loop(0, HEADS, one_head, 0)
+def attend(q_ref, k_ref, v_ref, att_ref, key_ref, query_ref, value_ref, score_ref, top_ref, prob_ref):
+    key_ref[...] = k_ref[...].T
+    query_ref[...] = jnp.zeros_like(query_ref)
+    value_ref[...] = jnp.ones_like(value_ref)
+    parts = PATCH // COLS
+
+    def head_rows(h):
+        return pl.ds(pl.multiple_of(h * HD, HD), HD)
+
+    def score(h, part, slot):
+        if part == 0:
+            query_ref[h % 2, head_rows((h + HEADS - 2) % HEADS), :] = jnp.zeros((HD, PATCH), BF)
+            query_ref[h % 2, head_rows(h), :] = q_ref[head_rows(h), :]
+        scores = jnp.dot(
+            key_ref[...],
+            query_ref[h % 2, :, part * COLS : (part + 1) * COLS],
+            preferred_element_type=F32,
+        )
+        score_ref[slot] = scores
+        top_ref[slot] = jnp.broadcast_to(jnp.max(scores, axis=0, keepdims=True), (8, COLS))
+
+    score(0, 0, 0)
+
+    def two_heads(pair, _):
+        for unit in range(2 * parts):
+            h, part, slot = pair * 2 + unit // parts, unit % parts, unit % 2
+            after = unit + 1
+            score(jnp.minimum(pair * 2 + after // parts, HEADS - 1), after % parts, after % 2)
+            prob_ref[slot] = jnp.exp2((score_ref[slot] - top_ref[slot][:1]) * SCORE).astype(BF)
+            value_ref[h % 2, :HD, :] = v_ref[head_rows(h), :]
+            sums = jnp.dot(value_ref[h % 2], prob_ref[slot], preferred_element_type=F32)
+            att_ref[head_rows(h), part * COLS : (part + 1) * COLS] = (sums[:HD] / sums[HD:]).astype(BF)
+        return 0
+
+    lax.fori_loop(0, HEADS // 2, two_heads, 0)
 
 
 def lanes_of(table_ref, group, rows):
@@ -238,8 +275,8 @@
     land_out, land_in, cell_out, cell_in,
     spread_ref, first_out, first_in, acc_ref,
     patch_out, patch_in, weights_ref,
-    x_ref, q_ref, k_ref, v_ref, km_ref, vm_ref, att_ref,
-    both_out, both_in, second_out, second_in,
+    x_ref, q_ref, k_ref, v_ref, att_ref, key_ref, query_ref, value_ref, score_ref, top_ref, prob_ref,
+    block_out, block_in, stat_out, stat_in, second_out, second_in,
     sum_ref, count_ref, mean_out, mean_in, table_out, table_in,
     turned_ref, back_out, back_in,
     wide_send, wide_recv, narrow_send, narrow_recv,
@@ -260,7 +297,8 @@
     back = wide(4, back_out, back_in, -1)
     gather = narrow(0, own_ref, weights_ref, True)
     patches = narrow(1, patch_out, patch_in)
-    boths = narrow(2, both_out, both_in)
+    blocks = narrow(2, block_out, block_in)
+    stats = narrow(5, stat_out, stat_in, True)
     means = narrow(3, mean_out, mean_in)
     tables = narrow(4, table_out, table_in)
 
@@ -287,32 +325,33 @@
     lax.fori_loop(1, GROUPS, greet_wide, 0)
     lax.fori_loop(1, BANDS, greet_narrow, 0)
 
-    position = hilbert_ref[...]
-    make_slots(
-        HROWS, ((position >> 13) - me) & (GROUPS - 1), position & (POINTS - 1), row_ref, low_ref, land_out
-    )
+    rank_points(HROWS, 13, hilbert_ref, row_ref, low_ref)
     for j in range(BANDS):
         at = slice(j * PATCH, (j + 1) * PATCH)
         spread_ref[:, at] = spread(feats_ref[:, at], low_ref[j : j + 1, :])
-    pl.semaphore_wait(barrier, GROUPS + BANDS - 2)
-    gather.start()
-    for g in range(4):
-        landings.start(g)
 
     def first_block(g, _):
         chunk = place(row_ref, spread_ref, g * 512, 512).astype(BF)
         first_out[pl.ds(g * 8, 8)] = chunk.reshape(8, HROWS, LO * CH)
+
+        @pl.when(g == 0)
+        def _():
+            pl.semaphore_wait(barrier, GROUPS + BANDS - 2)
+
         first.start(g)
+
+        @pl.when(g == 0)
+        def _():
+            make_table(HROWS, 13, hilbert_ref, row_ref, low_ref, land_out)
+            lax.fori_loop(0, 4, lambda i, _: landings.start(i) or 0, 0)
+
         return 0
 
     lax.fori_loop(0, 4, first_block, 0)
-
-    cell = cell_ref[...]
-    make_slots(
-        PROWS, ((cell >> 11) - me) & (GROUPS - 1), cell & (CELLS - 1), p_row_ref, p_low_ref, cell_out
-    )
-    for g in range(4):
-        cells.start(g)
+    gather.start()
+    rank_points(PROWS, 11, cell_ref, p_row_ref, p_low_ref)
+    make_table(PROWS, 11, cell_ref, p_row_ref, p_low_ref, cell_out)
+    lax.fori_loop(0, 4, lambda i, _: cells.start(i) or 0, 0)
 
     def first_group(g, _):
         landings.wait(g)
@@ -348,7 +387,9 @@
         turned = patch_in[n].T
         for l in range(LO):
             x_ref[n * CH : (n + 1) * CH, l * 128 : (l + 1) * 128] = turned[l * CH : (l + 1) * CH]
-    normed = normalise(x_ref[...].astype(F32), gain_ref)
+    gains = jnp.broadcast_to(gain_ref[...], (8, C)).T[:, :1]
+    wide_x = x_ref[...].astype(F32)
+    normed = normalise(wide_x, *statistics(wide_x), gains)
 
     def weight(start):
         return jnp.concatenate([weights_ref[n, start : start + CH, :] for n in range(BANDS)], axis=0)
@@ -356,24 +397,33 @@
     def project(t):
         return jnp.dot(weight(t * CH), normed, preferred_element_type=F32).astype(BF)
 
-    q_ref[...] = project(0).T
+    q_ref[...] = project(0)
     k_ref[...] = project(1)
-    v_ref[...] = project(2).T
-    attend(x_ref, q_ref, k_ref, v_ref, km_ref, vm_ref, att_ref)
-    added = lax.dot_general(
-        weight(3 * CH).T, att_ref[...].astype(BF), NT, preferred_element_type=F32
+    v_ref[...] = project(2)
+    attend(
+        q_ref, k_ref, v_ref, att_ref, key_ref, query_ref, value_ref, score_ref, top_ref, prob_ref
     )
+    added = jnp.dot(weight(3 * CH).T, att_ref[...], preferred_element_type=F32)
     block = (x_ref[...].astype(F32) + added).astype(BF)
-    pooled = normalise(block.astype(F32), gain2_ref)
+    block_out[...] = block.reshape(BANDS, CH, PATCH)
+    blocks.start()
+    average, scale = statistics(block.astype(F32))
+    stat_out[:1, :] = average
+    stat_out[1:, :] = scale
+    stats.start()
+    stats.wait()
+    blocks.wait()
+
+    gains2 = jnp.broadcast_to(gain2_ref[...], (8, C)).T[:, :1].reshape(BANDS, CH, 1)
+    gain2 = jnp.zeros((CH, 1), F32)
     for n in range(BANDS):
-        both_out[n, :CH, :] = pooled[n * CH : (n + 1) * CH]
-        both_out[n, CH:, :] = block[n * CH : (n + 1) * CH]
-    boths.start()
-    boths.wait()
-
+        gain2 = jnp.where(mine == n, gains2[n], gain2)
     for j in range(BANDS):
         at = slice(j * PATCH, (j + 1) * PATCH)
-        spread_ref[:, at] = spread(both_in[j, :CH, :], p_low_ref[j : j + 1, :])
+        pooled = normalise(
+            block_in[j].astype(F32), stat_in[j, :1, :], stat_in[j, 1:, :], gain2
+        )
+        spread_ref[:, at] = spread(pooled, p_low_ref[j : j + 1, :])
 
     def second_block(g, _):
         chunk = place(p_row_ref, spread_ref, g * 384, 384).astype(BF)
@@ -383,7 +433,7 @@
 
     lax.fori_loop(0, 4, second_block, 0)
     for j in range(BANDS):
-        block_ref[:, j * PATCH : (j + 1) * PATCH] = both_in[j, CH:, :]
+        block_ref[:, j * PATCH : (j + 1) * PATCH] = block_in[j]
     sum_ref[...] = jnp.zeros_like(sum_ref)
     count_ref[...] = jnp.zeros_like(count_ref)
     k = 8 * PROWS
@@ -466,7 +516,7 @@
         return 0
 
     lax.fori_loop(0, 4, take_group, 0)
-    for each in (landings, first, cells, second, back, gather, patches, boths, means, tables):
+    for each in (landings, first, cells, second, back, gather, patches, blocks, stats, means, tables):
         each.finish()
 
 
@@ -494,9 +544,11 @@
                 full(PATCH, LO * CH),
                 half(BANDS, PATCH // LO, LO * CH), half(BANDS, PATCH // LO, LO * CH),
                 half(BANDS, 6 * CH, C),
-                half(C, PATCH), half(PATCH, C), half(C, PATCH), half(PATCH, C),
-                half(C, PATCH), half(PATCH, C), full(PATCH, C),
-                half(BANDS, 2 * CH, PATCH), half(BANDS, 2 * CH, PATCH),
+                half(C, PATCH), half(C, PATCH), half(C, PATCH), half(C, PATCH), half(C, PATCH),
+                half(PATCH, C), half(2, C, PATCH), half(2, 2 * HD, PATCH),
+                full(2, PATCH, COLS), full(2, 8, COLS), half(2, PATCH, COLS),
+                half(BANDS, CH, PATCH), half(BANDS, CH, PATCH),
+                full(2, PATCH), full(BANDS, 2, PATCH),
                 half(GROUPS, PROWS, LO * CH), half(GROUPS, PROWS, LO * CH),
                 full(CHI, LO * CH), full(CHI, LO * CH),
                 full(BANDS, CH, CHI), full(BANDS, CH, CHI),
@@ -504,18 +556,18 @@
                 half(LO * CH2, 8 * PROWS),
                 half(GROUPS, PROWS, LO * CH2), half(GROUPS, PROWS, LO * CH2),
                 pltpu.SemaphoreType.DMA((5, GROUPS)), pltpu.SemaphoreType.DMA((5, GROUPS)),
-                pltpu.SemaphoreType.DMA((5, BANDS)), pltpu.SemaphoreType.DMA((5, BANDS)),
+                pltpu.SemaphoreType.DMA((6, BANDS)), pltpu.SemaphoreType.DMA((6, BANDS)),
             ],
             compiler_params=pltpu.CompilerParams(
                 collective_id=0, has_side_effects=True, vmem_limit_bytes=56 * 1024 * 1024
             ),
         )(
             feats,
-            hilbert_pos.reshape(BANDS, PATCH),
-            cell_of.reshape(BANDS, PATCH),
+            hilbert_pos.reshape(1, POINTS),
+            cell_of.reshape(1, POINTS),
             own,
-            ln_attn.reshape(C, 1),
-            ln_pool.reshape(C, 1),
+            ln_attn.reshape(1, C),
+            ln_pool.reshape(1, C),
         )
     )
 

time: 205 us -> 176 us (0.86)
  the two profiles are of different devices: /device:TPU:96 before, /device:TPU:1 now
where the time goes in v1:
time: 176 us
  Pallas kernels  169 us (96%)
  local copies, waits for them, and re-layouts  4.6 us (3%)
    pallas_call x1, Pallas kernels, on_device(): pl.pallas_call(kernel, out_shape=[jax.ShapeDtypeStruct((CH, POINTS), BF),...  169 us
    unnamed x5, local copies, waits for them, and re-layouts  4.6 us

profile of v1, /device:TPU:1, one launch (start us, length us, event | category | flops | bytes accessed | tf_op | source)
XLA Modules:
  0.0 175.6 jit_solution(14241477723101220010)
XLA Ops:
  0.6 1.5 pad_maximum_fusion.own_ref
  2.1 168.9 %shard_map.103 = (bf16[32,8192]{1,0:T(8,128)(2,1)}, bf16[64,2048]{1,0:T(8,128)(2,1)}, bf16[64,8192]{1,0:T(8,128)(2,1)}) custom-call(bf16[32,8192]{1,0:T(8,128)(2,1)} %feats_ref.1, s32[1,8192]{1,0:T(1,128)} %bitcast.10, s32[1,8192]{1,0:T(1,128)} %bitcast.11, bf16[192,256]{1,0:T(8,128)(2,1)} %pad_maximum_fusion.own_ref, f32[1,256]{1,0:T(1,128)} %bitcast.12, ...), custom_call_target="tpu_custom_call" | custom-call | tf_op jit(solution)/shard_map/pallas_call | solution.py:530
  171.0 0.0 copy-start
  171.0 2.0 %copy.14 = bf16[32,8192]{1,0:T(8,128)(2,1)} copy(bf16[32,8192]{1,0:T(8,128)(2,1)} %get-tuple-element.6) | data formatting | bytes 1048576
  173.0 1.7 copy.15
  174.7 0.0 copy-done
  174.7 1.0 copy.16
Async XLA Ops:
  171.0 3.6 %copy-start = (bf16[64,8192]{1,0:T(8,128)(2,1)S(1)}, bf16[64,8192]{1,0:T(8,128)(2,1)}, u32[]{:S(2)}) copy-start(bf16[64,8192]{1,0:T(8,128)(2,1)} %get-tuple-element.8) | copy-start | bytes 3145732

commit v2 on v1

--- a/solution.py
+++ b/solution.py
@@ -19,6 +19,9 @@
 LO = 8
 TAB = 128
 OWN = 1
+RELAYED = (2, 6)
+ANY = pl.BlockSpec(memory_space=pl.ANY)
+INSIDE = pl.BlockSpec(memory_space=pltpu.VMEM)
 COLS = 512
 HROWS = 64
 PROWS = 48
@@ -146,42 +149,86 @@
 
 
 class Wide:
-    def __init__(self, src, dst, send_sem, recv_sem, sign):
+    def __init__(self, src, dst, send_sem, recv_sem, sign, relay=None, relay_send=None, relay_recv=None):
         self.src, self.dst, self.send_sem, self.recv_sem, self.sign = src, dst, send_sem, recv_sem, sign
-
-    def each(self, first, count, act):
+        self.relay, self.relay_send, self.relay_recv = relay, relay_send, relay_recv
+
+    def copy(self, t):
+        return remote(
+            self.src.at[t],
+            self.dst.at[t],
+            self.send_sem.at[t],
+            self.recv_sem.at[t],
+            partner(t, self.sign),
+            lax.axis_index("narrow"),
+        )
+
+    def hop(self, k):
+        me = lax.axis_index("wide")
+        return remote(
+            self.src.at[RELAYED[k]],
+            self.relay.at[k],
+            self.send_sem.at[RELAYED[k]],
+            self.relay_recv.at[k],
+            (me // 4 + 7) % 8 * 4 + me % 4,
+            lax.axis_index("narrow"),
+        )
+
+    def second_hop(self, k):
+        me = lax.axis_index("wide")
+        across = RELAYED[k] // 2
+        return remote(
+            self.relay.at[k],
+            self.dst.at[RELAYED[k]],
+            self.relay_send.at[k],
+            self.recv_sem.at[RELAYED[k]],
+            (me // 4 + 5) % 8 * 4 + (me % 4 + self.sign * across + 4) % 4,
+            lax.axis_index("narrow"),
+        )
+
+    def each(self, first, count, act, skip=()):
         def one(i, _):
             t = first + i
-
-            @pl.when(t != OWN)
+            takes = t != OWN
+            for other in skip:
+                takes = takes & (t != other)
+
+            @pl.when(takes)
             def _():
-                act(
-                    remote(
-                        self.src.at[t],
-                        self.dst.at[t],
-                        self.send_sem.at[t],
-                        self.recv_sem.at[t],
-                        partner(t, self.sign),
-                        lax.axis_index("narrow"),
-                    )
-                )
+                act(self.copy(t))
 
             return 0
 
         lax.fori_loop(0, count, one, 0)
 
     def start(self, group):
-        self.each(group * 8, 8, lambda copy: copy.start())
-
-        @pl.when(group == OWN // 8)
+        relayed = RELAYED if self.relay is not None else ()
+
+        @pl.when(group == 0)
         def _():
+            for k in range(len(relayed)):
+                self.hop(k).start()
             self.dst[OWN] = self.src[OWN]
+
+        self.each(group * 8, 8, lambda copy: copy.start(), relayed)
+
+    def forward(self):
+        for k in range(len(RELAYED)):
+            self.hop(k).wait_recv()
+            self.second_hop(k).start()
 
     def wait(self, group):
         self.each(group * 8, 8, lambda copy: copy.wait_recv())
 
     def finish(self):
         self.each(0, GROUPS, lambda copy: copy.wait_send())
+        if self.relay is not None:
+            for k in range(len(RELAYED)):
+                self.second_hop(k).wait_send()
+
+
+def arrival(i):
+    return i // 3 * 3 + (1 - i // 3) * ((i + 1) % 3)
 
 
 class Narrow:
@@ -205,6 +252,24 @@
         me = lax.axis_index("narrow")
         lax.fori_loop(1, BANDS, lambda s, _: self.copy(s).start() or 0, 0)
         self.dst[me] = self.src[...] if self.whole else self.src[me]
+
+    def start_half(self, half):
+        me = lax.axis_index("narrow")
+
+        def one(i, _):
+            step = (half * 4 + i - me + BANDS) % BANDS
+
+            @pl.when(step != 0)
+            def _():
+                self.copy(step).start()
+
+            return 0
+
+        lax.fori_loop(0, 4, one, 0)
+
+        @pl.when(me // 4 == half)
+        def _():
+            self.dst[me] = self.src[me]
 
     def wait(self):
         me = lax.axis_index("narrow")
@@ -227,41 +292,33 @@
         lax.fori_loop(1, BANDS, lambda s, _: self.copy(s).wait_send() or 0, 0)
 
 
-def attend(q_ref, k_ref, v_ref, att_ref, key_ref, query_ref, value_ref, score_ref, top_ref, prob_ref):
-    key_ref[...] = k_ref[...].T
-    query_ref[...] = jnp.zeros_like(query_ref)
-    value_ref[...] = jnp.ones_like(value_ref)
-    parts = PATCH // COLS
+def attend(part, q_ref, k_ref, v_ref, att_ref, key_ref, query_ref, value_ref, score_ref, top_ref, prob_ref):
+    columns = slice(part * COLS, (part + 1) * COLS)
 
     def head_rows(h):
         return pl.ds(pl.multiple_of(h * HD, HD), HD)
 
-    def score(h, part, slot):
-        if part == 0:
-            query_ref[h % 2, head_rows((h + HEADS - 2) % HEADS), :] = jnp.zeros((HD, PATCH), BF)
-            query_ref[h % 2, head_rows(h), :] = q_ref[head_rows(h), :]
-        scores = jnp.dot(
-            key_ref[...],
-            query_ref[h % 2, :, part * COLS : (part + 1) * COLS],
-            preferred_element_type=F32,
-        )
+    def score(h, slot):
+        query_ref[slot, head_rows((h + HEADS - 2) % HEADS), :] = jnp.zeros((HD, COLS), BF)
+        query_ref[slot, head_rows(h), :] = q_ref[head_rows(h), columns]
+        scores = jnp.dot(key_ref[...], query_ref[slot], preferred_element_type=F32)
         score_ref[slot] = scores
         top_ref[slot] = jnp.broadcast_to(jnp.max(scores, axis=0, keepdims=True), (8, COLS))
 
-    score(0, 0, 0)
-
-    def two_heads(pair, _):
-        for unit in range(2 * parts):
-            h, part, slot = pair * 2 + unit // parts, unit % parts, unit % 2
-            after = unit + 1
-            score(jnp.minimum(pair * 2 + after // parts, HEADS - 1), after % parts, after % 2)
+    query_ref[...] = jnp.zeros_like(query_ref)
+    score(0, 0)
+
+    def four_heads(quad, _):
+        for unit in range(4):
+            h, slot = quad * 4 + unit, unit % 2
+            score(jnp.minimum(h + 1, HEADS - 1), 1 - slot)
             prob_ref[slot] = jnp.exp2((score_ref[slot] - top_ref[slot][:1]) * SCORE).astype(BF)
-            value_ref[h % 2, :HD, :] = v_ref[head_rows(h), :]
-            sums = jnp.dot(value_ref[h % 2], prob_ref[slot], preferred_element_type=F32)
-            att_ref[head_rows(h), part * COLS : (part + 1) * COLS] = (sums[:HD] / sums[HD:]).astype(BF)
-        return 0
-
-    lax.fori_loop(0, HEADS // 2, two_heads, 0)
+            value_ref[slot, :HD, :] = v_ref[head_rows(h), :]
+            sums = jnp.dot(value_ref[slot], prob_ref[slot], preferred_element_type=F32)
+            att_ref[head_rows(h), columns] = (sums[:HD] / sums[HD:]).astype(BF)
+        return 0
+
+    lax.fori_loop(0, HEADS // 4, four_heads, 0)
 
 
 def lanes_of(table_ref, group, rows):
@@ -269,8 +326,9 @@
 
 
 def kernel(
-    feats_ref, hilbert_ref, cell_ref, own_ref, gain_ref, gain2_ref,
-    block_ref, coarse_ref, unpooled_ref,
+    feats_ref, hilbert_ref, cell_ref, qkv_ref, proj_ref, pool_ref, gain_ref, gain2_ref,
+    block_goal, coarse_goal, unpooled_goal,
+    block_ref, coarse_ref, unpooled_ref, own_ref,
     row_ref, low_ref, p_row_ref, p_low_ref,
     land_out, land_in, cell_out, cell_in,
     spread_ref, first_out, first_in, acc_ref,
@@ -279,28 +337,32 @@
     block_out, block_in, stat_out, stat_in, second_out, second_in,
     sum_ref, count_ref, mean_out, mean_in, table_out, table_in,
     turned_ref, back_out, back_in,
-    wide_send, wide_recv, narrow_send, narrow_recv,
+    first_relay, second_relay, back_relay, relay_send, relay_recv,
+    wide_send, wide_recv, narrow_send, narrow_recv, goal_sem,
 ):
     me = lax.axis_index("wide")
     mine = lax.axis_index("narrow")
 
-    def wide(number, src, dst, sign=1):
-        return Wide(src, dst, wide_send.at[number], wide_recv.at[number], sign)
+    def wide(number, src, dst, sign=1, relay=None):
+        return Wide(
+            src, dst, wide_send.at[number], wide_recv.at[number], sign,
+            relay, relay_send.at[number], relay_recv.at[number],
+        )
 
     def narrow(number, src, dst, whole=False):
         return Narrow(src, dst, narrow_send.at[number], narrow_recv.at[number], whole)
 
     landings = wide(0, land_out, land_in)
-    first = wide(1, first_out, first_in)
+    first = wide(1, first_out, first_in, 1, first_relay)
     cells = wide(2, cell_out, cell_in)
-    second = wide(3, second_out, second_in)
-    back = wide(4, back_out, back_in, -1)
+    second = wide(3, second_out, second_in, 1, second_relay)
+    back = wide(4, back_out, back_in, -1, back_relay)
     gather = narrow(0, own_ref, weights_ref, True)
     patches = narrow(1, patch_out, patch_in)
-    blocks = narrow(2, block_out, block_in)
-    stats = narrow(5, stat_out, stat_in, True)
-    means = narrow(3, mean_out, mean_in)
-    tables = narrow(4, table_out, table_in)
+    blocks = [narrow(2 + i, block_out.at[i], block_in.at[i]) for i in range(2)]
+    stats = [narrow(6 + i, stat_out.at[i], stat_in.at[i], True) for i in range(2)]
+    means = narrow(4, mean_out, mean_in)
+    tables = narrow(5, table_out, table_in)
 
     barrier = pltpu.get_barrier_semaphore()
 
@@ -325,6 +387,10 @@
     lax.fori_loop(1, GROUPS, greet_wide, 0)
     lax.fori_loop(1, BANDS, greet_narrow, 0)
 
+    own_ref[: 3 * CH, :] = qkv_ref[...]
+    own_ref[3 * CH : 4 * CH, :] = proj_ref[...]
+    own_ref[4 * CH :, :] = pool_ref[...]
+
     rank_points(HROWS, 13, hilbert_ref, row_ref, low_ref)
     for j in range(BANDS):
         at = slice(j * PATCH, (j + 1) * PATCH)
@@ -337,6 +403,10 @@
         @pl.when(g == 0)
         def _():
             pl.semaphore_wait(barrier, GROUPS + BANDS - 2)
+
+        @pl.when(g == 2)
+        def _():
+            first.forward()
 
         first.start(g)
 
@@ -353,7 +423,8 @@
     make_table(PROWS, 11, cell_ref, p_row_ref, p_low_ref, cell_out)
     lax.fori_loop(0, 4, lambda i, _: cells.start(i) or 0, 0)
 
-    def first_group(g, _):
+    def first_group(i, _):
+        g = arrival(i)
         landings.wait(g)
         first.wait(g)
         k = 8 * HROWS
@@ -374,12 +445,17 @@
                     preferred_element_type=F32,
                 )
             at = slice(m * 512, (m + 1) * 512)
-            acc_ref[at, :] = jnp.where(g == 0, total, total + acc_ref[at, :])
+            total = jnp.where(i == 0, total, total + acc_ref[at, :])
+            acc_ref[at, :] = total
+
+            @pl.when(i == 3)
+            def _():
+                patch_out[m * 4 : (m + 1) * 4] = total.astype(BF).reshape(4, PATCH // LO, LO * CH)
+                patches.start_half(m)
+
         return 0
 
     lax.fori_loop(0, 4, first_group, 0)
-    patch_out[...] = acc_ref[...].astype(BF).reshape(BANDS, PATCH // LO, LO * CH)
-    patches.start()
     gather.wait()
     patches.wait()
 
@@ -400,40 +476,55 @@
     q_ref[...] = project(0)
     k_ref[...] = project(1)
     v_ref[...] = project(2)
-    attend(
-        q_ref, k_ref, v_ref, att_ref, key_ref, query_ref, value_ref, score_ref, top_ref, prob_ref
-    )
-    added = jnp.dot(weight(3 * CH).T, att_ref[...], preferred_element_type=F32)
-    block = (x_ref[...].astype(F32) + added).astype(BF)
-    block_out[...] = block.reshape(BANDS, CH, PATCH)
-    blocks.start()
-    average, scale = statistics(block.astype(F32))
-    stat_out[:1, :] = average
-    stat_out[1:, :] = scale
-    stats.start()
-    stats.wait()
-    blocks.wait()
+    key_ref[...] = k_ref[...].T
+    value_ref[...] = jnp.ones_like(value_ref)
+    proj = weight(3 * CH).T
+    for part in range(2):
+        attend(
+            part, q_ref, k_ref, v_ref, att_ref, key_ref, query_ref, value_ref, score_ref, top_ref, prob_ref
+        )
+        columns = slice(part * COLS, (part + 1) * COLS)
+        added = jnp.dot(proj, att_ref[:, columns], preferred_element_type=F32)
+        block = (x_ref[:, columns].astype(F32) + added).astype(BF)
+        block_out[part] = block.reshape(BANDS, CH, COLS)
+        blocks[part].start()
+        average, scale = statistics(block.astype(F32))
+        stat_out[part, :1, :] = average
+        stat_out[part, 1:, :] = scale
+        stats[part].start()
 
     gains2 = jnp.broadcast_to(gain2_ref[...], (8, C)).T[:, :1].reshape(BANDS, CH, 1)
     gain2 = jnp.zeros((CH, 1), F32)
     for n in range(BANDS):
         gain2 = jnp.where(mine == n, gains2[n], gain2)
-    for j in range(BANDS):
-        at = slice(j * PATCH, (j + 1) * PATCH)
-        pooled = normalise(
-            block_in[j].astype(F32), stat_in[j, :1, :], stat_in[j, 1:, :], gain2
-        )
-        spread_ref[:, at] = spread(pooled, p_low_ref[j : j + 1, :])
+    for part in range(2):
+        stats[part].wait()
+        blocks[part].wait()
+        for j in range(BANDS):
+            at = slice(j * PATCH + part * COLS, j * PATCH + (part + 1) * COLS)
+            pooled = normalise(
+                block_in[part, j].astype(F32), stat_in[part, j, :1, :], stat_in[part, j, 1:, :], gain2
+            )
+            spread_ref[:, at] = spread(pooled, p_low_ref[j : j + 1, part * COLS : (part + 1) * COLS])
 
     def second_block(g, _):
         chunk = place(p_row_ref, spread_ref, g * 384, 384).astype(BF)
         second_out[pl.ds(g * 8, 8)] = chunk.reshape(8, PROWS, LO * CH)
+
+        @pl.when(g == 2)
+        def _():
+            second.forward()
+
         second.start(g)
         return 0
 
     lax.fori_loop(0, 4, second_block, 0)
     for j in range(BANDS):
-        block_ref[:, j * PATCH : (j + 1) * PATCH] = block_in[j]
+        for part in range(2):
+            at = slice(j * PATCH + part * COLS, j * PATCH + (part + 1) * COLS)
+            block_ref[:, at] = block_in[part, j]
+    block_leaves = pltpu.make_async_copy(block_ref, block_goal, goal_sem.at[0])
+    block_leaves.start()
     sum_ref[...] = jnp.zeros_like(sum_ref)
     count_ref[...] = jnp.zeros_like(count_ref)
     k = 8 * PROWS
@@ -453,7 +544,8 @@
 
     lax.fori_loop(0, 4, count_group, 0)
 
-    def second_group(g, _):
+    def second_group(i, _):
+        g = arrival(i)
         second.wait(g)
         turned = second_in[pl.ds(g * 8, 8)].reshape(k, LO * CH).T
         cell = lanes_of(cell_in, g, PROWS)
@@ -495,15 +587,23 @@
                 product, cell[l : l + 1] >> 8, CH2
             ).astype(BF)
         back_out[pl.ds(g * 8, 8)] = turned_ref[...].T.reshape(8, PROWS, LO * CH2)
+
+        @pl.when(g == 2)
+        def _():
+            back.forward()
+
         back.start(g)
         return 0
 
     lax.fori_loop(0, 4, give_group, 0)
     for n in range(BANDS):
         coarse_ref[:, n * CHI : (n + 1) * CHI] = table_in[n]
+    coarse_leaves = pltpu.make_async_copy(coarse_ref, coarse_goal, goal_sem.at[1])
+    coarse_leaves.start()
     unpooled_ref[...] = jnp.zeros_like(unpooled_ref)
 
-    def take_group(g, _):
+    def take_group(i, _):
+        g = arrival(i)
         back.wait(g)
         turned_ref[...] = back_in[pl.ds(g * 8, 8)].reshape(k, LO * CH2).T
         for j in range(BANDS):
@@ -516,27 +616,53 @@
         return 0
 
     lax.fori_loop(0, 4, take_group, 0)
-    for each in (landings, first, cells, second, back, gather, patches, blocks, stats, means, tables):
+    unpooled_leaves = pltpu.make_async_copy(unpooled_ref, unpooled_goal, goal_sem.at[2])
+    unpooled_leaves.start()
+    for each in (landings, first, cells, second, back, gather, patches, *blocks, *stats, means, tables):
         each.finish()
+    block_leaves.wait()
+    coarse_leaves.wait()
+    unpooled_leaves.wait()
+
+
+def settle_kernel(a_ref, b_ref, c_ref, a_out, b_out, c_out, sem):
+    copies = [
+        pltpu.make_async_copy(a_ref, a_out, sem.at[0]),
+        pltpu.make_async_copy(b_ref, b_out, sem.at[1]),
+        pltpu.make_async_copy(c_ref, c_out, sem.at[2]),
+    ]
+    for copy in copies:
+        copy.start()
+    for copy in copies:
+        copy.wait()
 
 
 def on_device(feats, hilbert_pos, ln_attn, w_qkv, w_proj, ln_pool, w_pool, cell_of):
-    own = jnp.concatenate([w_qkv.transpose(0, 2, 1).reshape(-1, C), w_proj, w_pool.T], axis=0)
     small = lambda: pltpu.VMEM((BANDS, PATCH), jnp.int32)
     table = lambda: pltpu.VMEM((GROUPS, LO, TAB), jnp.int32)
     half = lambda *dims: pltpu.VMEM(dims, BF)
     full = lambda *dims: pltpu.VMEM(dims, F32)
+    results = [
+        jax.ShapeDtypeStruct((CH, POINTS), BF),
+        jax.ShapeDtypeStruct((CH2, CELLS), BF),
+        jax.ShapeDtypeStruct((CH2, POINTS), BF),
+    ]
+    settle = pl.pallas_call(
+        settle_kernel,
+        out_shape=results,
+        in_specs=[ANY] * 3,
+        out_specs=[ANY] * 3,
+        scratch_shapes=[pltpu.SemaphoreType.DMA((3,))],
+        compiler_params=pltpu.CompilerParams(vmem_limit_bytes=60 * 1024 * 1024),
+    )
     return tuple(
-        pl.pallas_call(
+        settle(*pl.pallas_call(
             kernel,
-            out_shape=[
-                jax.ShapeDtypeStruct((CH, POINTS), BF),
-                jax.ShapeDtypeStruct((CH2, CELLS), BF),
-                jax.ShapeDtypeStruct((CH2, POINTS), BF),
-            ],
-            in_specs=[pl.BlockSpec(memory_space=pltpu.VMEM)] * 6,
-            out_specs=[pl.BlockSpec(memory_space=pltpu.VMEM)] * 3,
+            out_shape=results,
+            in_specs=[INSIDE] * 8,
+            out_specs=[ANY] * 3,
             scratch_shapes=[
+                half(CH, POINTS), half(CH2, CELLS), half(CH2, POINTS), half(6 * CH, C),
                 small(), small(), small(), small(),
                 table(), table(), table(), table(),
                 half(LO * CH, POINTS),
@@ -545,18 +671,21 @@
                 half(BANDS, PATCH // LO, LO * CH), half(BANDS, PATCH // LO, LO * CH),
                 half(BANDS, 6 * CH, C),
                 half(C, PATCH), half(C, PATCH), half(C, PATCH), half(C, PATCH), half(C, PATCH),
-                half(PATCH, C), half(2, C, PATCH), half(2, 2 * HD, PATCH),
+                half(PATCH, C), half(2, C, COLS), half(2, 2 * HD, PATCH),
                 full(2, PATCH, COLS), full(2, 8, COLS), half(2, PATCH, COLS),
-                half(BANDS, CH, PATCH), half(BANDS, CH, PATCH),
-                full(2, PATCH), full(BANDS, 2, PATCH),
+                half(2, BANDS, CH, COLS), half(2, BANDS, CH, COLS),
+                full(2, 2, COLS), full(2, BANDS, 2, COLS),
                 half(GROUPS, PROWS, LO * CH), half(GROUPS, PROWS, LO * CH),
                 full(CHI, LO * CH), full(CHI, LO * CH),
                 full(BANDS, CH, CHI), full(BANDS, CH, CHI),
                 half(BANDS, CH2, CHI), half(BANDS, CH2, CHI),
                 half(LO * CH2, 8 * PROWS),
                 half(GROUPS, PROWS, LO * CH2), half(GROUPS, PROWS, LO * CH2),
+                half(2, HROWS, LO * CH), half(2, PROWS, LO * CH), half(2, PROWS, LO * CH2),
+                pltpu.SemaphoreType.DMA((5, 2)), pltpu.SemaphoreType.DMA((5, 2)),
                 pltpu.SemaphoreType.DMA((5, GROUPS)), pltpu.SemaphoreType.DMA((5, GROUPS)),
-                pltpu.SemaphoreType.DMA((6, BANDS)), pltpu.SemaphoreType.DMA((6, BANDS)),
+                pltpu.SemaphoreType.DMA((8, BANDS)), pltpu.SemaphoreType.DMA((8, BANDS)),
+                pltpu.SemaphoreType.DMA((3,)),
             ],
             compiler_params=pltpu.CompilerParams(
                 collective_id=0, has_side_effects=True, vmem_limit_bytes=56 * 1024 * 1024
@@ -565,10 +694,12 @@
             feats,
             hilbert_pos.reshape(1, POINTS),
             cell_of.reshape(1, POINTS),
-            own,
+            w_qkv.transpose(0, 2, 1).reshape(-1, C),
+            w_proj,
+            w_pool.T,
             ln_attn.reshape(1, C),
             ln_pool.reshape(1, C),
-        )
+        ))
     )
 
 

time: 176 us -> 250 us (1.42)
  Pallas kernels: 169 us -> 249 us
  local copies, waits for them, and re-layouts: 4.6 us -> 0 us
    pallas_call x1 -> x2, Pallas kernels: 169 us -> 249 us  [the longest x1 192 us: on_device(): pl.pallas_call(kernel, out_shape=results, in_specs=[INSIDE] * 8, out_spec...]
    unnamed x5 -> x0, local copies, waits for them, and re-layouts: 4.6 us -> none
where the time goes in v2:
time: 250 us
  Pallas kernels  249 us (100%)
    pallas_call x1, Pallas kernels, on_device(): pl.pallas_call(kernel, out_shape=results, in_specs=[INSIDE] * 8, out_spec...  192 us
    pallas_call x1, Pallas kernels, on_device(): settle(*pl.pallas_call(kernel, out_shape=results, in_specs=[INSIDE] * 8,...  56.7 us

profile of v2, /device:TPU:1, one launch (start us, length us, event | category | flops | bytes accessed | tf_op | source)
XLA Modules:
  0.0 249.6 jit_solution(12266147845620097436)
XLA Ops:
  0.6 192.1 %shard_map.103 = (bf16[32,8192]{1,0:T(8,128)(2,1)}, bf16[64,2048]{1,0:T(8,128)(2,1)}, bf16[64,8192]{1,0:T(8,128)(2,1)}) custom-call(bf16[32,8192]{1,0:T(8,128)(2,1)} %feats_ref.1, s32[1,8192]{1,0:T(1,128)} %bitcast.9, s32[1,8192]{1,0:T(1,128)} %bitcast.10, bf16[96,256]{1,0:T(8,128)(2,1)} %bitcast.8, bf16[32,256]{1,0:T(8,128)(2,1)} %proj_ref.1, ...), custom_call_target="tpu_custom_call" | custom-call | tf_op jit(solution)/shard_map/pallas_call | solution.py:659
  192.7 56.7 %shard_map.104 = (bf16[32,8192]{1,0:T(8,128)(2,1)}, bf16[64,2048]{1,0:T(8,128)(2,1)}, bf16[64,8192]{1,0:T(8,128)(2,1)}) custom-call(bf16[32,8192]{1,0:T(8,128)(2,1)} %get-tuple-element.6.a_ref, bf16[64,2048]{1,0:T(8,128)(2,1)} %get-tuple-element.7.b_ref, bf16[64,8192]{1,0:T(8,128)(2,1)} %get-tuple-element.8.c_ref), custom_call_target="tpu_custom_call" | custom-call | tf_op jit(solution)/shard_map/pallas_call | solution.py:659

commit v3 on v1

--- a/solution.py
+++ b/solution.py
@@ -19,6 +19,7 @@
 LO = 8
 TAB = 128
 OWN = 1
+INSIDE = pl.BlockSpec(memory_space=pltpu.VMEM)
 COLS = 512
 HROWS = 64
 PROWS = 48
@@ -206,6 +207,24 @@
         lax.fori_loop(1, BANDS, lambda s, _: self.copy(s).start() or 0, 0)
         self.dst[me] = self.src[...] if self.whole else self.src[me]
 
+    def start_half(self, half):
+        me = lax.axis_index("narrow")
+
+        def one(i, _):
+            step = (half * 4 + i - me + BANDS) % BANDS
+
+            @pl.when(step != 0)
+            def _():
+                self.copy(step).start()
+
+            return 0
+
+        lax.fori_loop(0, 4, one, 0)
+
+        @pl.when(me // 4 == half)
+        def _():
+            self.dst[me] = self.src[me]
+
     def wait(self):
         me = lax.axis_index("narrow")
 
@@ -264,21 +283,26 @@
     lax.fori_loop(0, HEADS // 2, two_heads, 0)
 
 
+def gelu(value):
+    return (value * (1.0 + lax.erf(value * (0.5**0.5))) * 0.5).astype(BF)
+
+
 def lanes_of(table_ref, group, rows):
     return jnp.concatenate([table_ref[group * 8 + i, :, :rows] for i in range(8)], axis=1)
 
 
 def kernel(
-    feats_ref, hilbert_ref, cell_ref, own_ref, gain_ref, gain2_ref,
-    block_ref, coarse_ref, unpooled_ref,
+    feats_ref, hilbert_ref, cell_ref, qkv_ref, proj_ref, pool_ref, gain_ref, gain2_ref,
+    block_in, table_in, result_in,
+    own_ref,
     row_ref, low_ref, p_row_ref, p_low_ref,
     land_out, land_in, cell_out, cell_in,
     spread_ref, first_out, first_in, acc_ref,
     patch_out, patch_in, weights_ref,
     x_ref, q_ref, k_ref, v_ref, att_ref, key_ref, query_ref, value_ref, score_ref, top_ref, prob_ref,
-    block_out, block_in, stat_out, stat_in, second_out, second_in,
-    sum_ref, count_ref, mean_out, mean_in, table_out, table_in,
-    turned_ref, back_out, back_in,
+    block_out, stat_out, stat_in, second_out, second_in,
+    sum_ref, count_ref, mean_ref, mean_in, table_out,
+    turned_ref, back_out, back_in, point_out, point_in, result_out,
     wide_send, wide_recv, narrow_send, narrow_recv,
 ):
     me = lax.axis_index("wide")
@@ -299,7 +323,9 @@
     patches = narrow(1, patch_out, patch_in)
     blocks = narrow(2, block_out, block_in)
     stats = narrow(5, stat_out, stat_in, True)
-    means = narrow(3, mean_out, mean_in)
+    points = narrow(6, point_out, point_in)
+    results = narrow(7, result_out, result_in)
+    means = narrow(3, mean_ref, mean_in)
     tables = narrow(4, table_out, table_in)
 
     barrier = pltpu.get_barrier_semaphore()
@@ -324,6 +350,10 @@
 
     lax.fori_loop(1, GROUPS, greet_wide, 0)
     lax.fori_loop(1, BANDS, greet_narrow, 0)
+
+    own_ref[: 3 * CH, :] = qkv_ref[...]
+    own_ref[3 * CH : 4 * CH, :] = proj_ref[...]
+    own_ref[4 * CH :, :] = pool_ref[...]
 
     rank_points(HROWS, 13, hilbert_ref, row_ref, low_ref)
     for j in range(BANDS):
@@ -374,12 +404,17 @@
                     preferred_element_type=F32,
                 )
             at = slice(m * 512, (m + 1) * 512)
-            acc_ref[at, :] = jnp.where(g == 0, total, total + acc_ref[at, :])
+            total = jnp.where(g == 0, total, total + acc_ref[at, :])
+            acc_ref[at, :] = total
+
+            @pl.when(g == 3)
+            def _():
+                patch_out[m * 4 : (m + 1) * 4] = total.astype(BF).reshape(4, PATCH // LO, LO * CH)
+                patches.start_half(m)
+
         return 0
 
     lax.fori_loop(0, 4, first_group, 0)
-    patch_out[...] = acc_ref[...].astype(BF).reshape(BANDS, PATCH // LO, LO * CH)
-    patches.start()
     gather.wait()
     patches.wait()
 
@@ -432,8 +467,6 @@
         return 0
 
     lax.fori_loop(0, 4, second_block, 0)
-    for j in range(BANDS):
-        block_ref[:, j * PATCH : (j + 1) * PATCH] = block_in[j]
     sum_ref[...] = jnp.zeros_like(sum_ref)
     count_ref[...] = jnp.zeros_like(count_ref)
     k = 8 * PROWS
@@ -467,76 +500,118 @@
         return 0
 
     lax.fori_loop(0, 4, second_group, 0)
-    mean_out[...] = (sum_ref[...] / jnp.maximum(count_ref[...], 1.0)).T.reshape(BANDS, CH, CHI)
+    mean = (sum_ref[...] / jnp.maximum(count_ref[...], 1.0)).T.astype(BF)
+    mean_ref[...] = mean.reshape(BANDS, CH, CHI)
+
+    def give_group(g, _):
+        cell = lanes_of(cell_in, g, PROWS)
+        means_of = mean_ref[...].reshape(C, CHI)
+        for l in range(LO):
+            product = jnp.dot(
+                means_of, one_hot(cell[l : l + 1] & (CHI - 1), 0, CHI), preferred_element_type=F32
+            )
+            turned_ref[l * CH : (l + 1) * CH, :] = gather_low(
+                product, cell[l : l + 1] >> 8, CH
+            ).astype(BF)
+        back_out[pl.ds(g * 8, 8)] = turned_ref[...].T.reshape(8, PROWS, LO * CH)
+        back.start(g)
+        return 0
+
+    lax.fori_loop(0, 4, give_group, 0)
     means.start()
     means.wait()
 
-    mean = mean_in[...].reshape(C, CHI)
-    upper = mean.astype(BF)
-    lower = (mean - upper.astype(F32)).astype(BF)
     for n in range(BANDS):
-        weight_n = weights_ref[n, 4 * CH :, :]
-        value = jnp.dot(weight_n, upper, preferred_element_type=F32) + jnp.dot(
-            weight_n, lower, preferred_element_type=F32
-        )
-        table_out[n] = (value * (1.0 + lax.erf(value * (0.5**0.5))) * 0.5).astype(BF)
+        table_out[n] = gelu(
+            jnp.dot(weights_ref[n, 4 * CH :, :], mean_in[...].reshape(C, CHI), preferred_element_type=F32)
+        )
     tables.start()
-    tables.wait()
-
-    table = table_in[...].reshape(BANDS * CH2, CHI)
-
-    def give_group(g, _):
-        cell = lanes_of(cell_in, g, PROWS)
-        for l in range(LO):
-            product = jnp.dot(
-                table, one_hot(cell[l : l + 1] & (CHI - 1), 0, CHI), preferred_element_type=F32
-            )
-            turned_ref[l * CH2 : (l + 1) * CH2, :] = gather_low(
-                product, cell[l : l + 1] >> 8, CH2
-            ).astype(BF)
-        back_out[pl.ds(g * 8, 8)] = turned_ref[...].T.reshape(8, PROWS, LO * CH2)
-        back.start(g)
-        return 0
-
-    lax.fori_loop(0, 4, give_group, 0)
-    for n in range(BANDS):
-        coarse_ref[:, n * CHI : (n + 1) * CHI] = table_in[n]
-    unpooled_ref[...] = jnp.zeros_like(unpooled_ref)
 
     def take_group(g, _):
         back.wait(g)
-        turned_ref[...] = back_in[pl.ds(g * 8, 8)].reshape(k, LO * CH2).T
-        for j in range(BANDS):
-            at = slice(j * PATCH, (j + 1) * PATCH)
-            product = jnp.dot(
-                turned_ref[...], one_hot(p_row_ref[j : j + 1, :], g * k, k), preferred_element_type=F32
+        turned_ref[...] = back_in[pl.ds(g * 8, 8)].reshape(k, LO * CH).T
+        for half_of in range(2):
+            for j in range(half_of * 4, half_of * 4 + 4):
+                product = jnp.dot(
+                    turned_ref[...],
+                    one_hot(p_row_ref[j : j + 1, :], g * k, k),
+                    preferred_element_type=F32,
+                )
+                part = gather_low(product, p_low_ref[j : j + 1, :], CH)
+                before = jnp.where(g == 0, 0.0, point_out[j].astype(F32))
+                point_out[j] = (before + part).astype(BF)
+
+            @pl.when(g == 3)
+            def _():
+                points.start_half(half_of)
+
+        return 0
+
+    point_out[...] = jnp.zeros_like(point_out)
+    lax.fori_loop(0, 4, take_group, 0)
+    points.wait()
+
+    def project_for(step, _):
+        n = (mine + step) % BANDS
+        result_out[n] = gelu(
+            jnp.dot(
+                weights_ref[n, 4 * CH :, :],
+                point_in[...].reshape(C, PATCH),
+                preferred_element_type=F32,
             )
-            part = gather_low(product, p_low_ref[j : j + 1, :], CH2)
-            unpooled_ref[:, at] = (unpooled_ref[:, at].astype(F32) + part).astype(BF)
-        return 0
-
-    lax.fori_loop(0, 4, take_group, 0)
-    for each in (landings, first, cells, second, back, gather, patches, blocks, stats, means, tables):
+        )
+
+        @pl.when(step != BANDS)
+        def _():
+            results.copy(step).start()
+
+        return 0
+
+    lax.fori_loop(1, BANDS + 1, project_for, 0)
+    result_in[mine] = result_out[mine]
+    results.wait()
+    tables.wait()
+    for each in (landings, first, cells, second, back):
         each.finish()
+    for each in (gather, patches, blocks, stats, means, tables, points, results):
+        each.finish()
+
+
+def settle_kernel(block_in, table_in, result_in, block_ref, coarse_ref, unpooled_ref):
+    for n in range(BANDS):
+        block_ref[:, n * PATCH : (n + 1) * PATCH] = block_in[n]
+        coarse_ref[:, n * CHI : (n + 1) * CHI] = table_in[n]
+        unpooled_ref[:, n * PATCH : (n + 1) * PATCH] = result_in[n]
 
 
 def on_device(feats, hilbert_pos, ln_attn, w_qkv, w_proj, ln_pool, w_pool, cell_of):
-    own = jnp.concatenate([w_qkv.transpose(0, 2, 1).reshape(-1, C), w_proj, w_pool.T], axis=0)
     small = lambda: pltpu.VMEM((BANDS, PATCH), jnp.int32)
     table = lambda: pltpu.VMEM((GROUPS, LO, TAB), jnp.int32)
     half = lambda *dims: pltpu.VMEM(dims, BF)
     full = lambda *dims: pltpu.VMEM(dims, F32)
+    settle = pl.pallas_call(
+        settle_kernel,
+        out_shape=[
+            jax.ShapeDtypeStruct((CH, POINTS), BF),
+            jax.ShapeDtypeStruct((CH2, CELLS), BF),
+            jax.ShapeDtypeStruct((CH2, POINTS), BF),
+        ],
+        in_specs=[INSIDE] * 3,
+        out_specs=[INSIDE] * 3,
+        compiler_params=pltpu.CompilerParams(vmem_limit_bytes=16 * 1024 * 1024),
+    )
     return tuple(
-        pl.pallas_call(
+        settle(*pl.pallas_call(
             kernel,
             out_shape=[
-                jax.ShapeDtypeStruct((CH, POINTS), BF),
-                jax.ShapeDtypeStruct((CH2, CELLS), BF),
-                jax.ShapeDtypeStruct((CH2, POINTS), BF),
+                jax.ShapeDtypeStruct((BANDS, CH, PATCH), BF),
+                jax.ShapeDtypeStruct((BANDS, CH2, CHI), BF),
+                jax.ShapeDtypeStruct((BANDS, CH2, PATCH), BF),
             ],
-            in_specs=[pl.BlockSpec(memory_space=pltpu.VMEM)] * 6,
-            out_specs=[pl.BlockSpec(memory_space=pltpu.VMEM)] * 3,
+            in_specs=[INSIDE] * 8,
+            out_specs=[INSIDE] * 3,
             scratch_shapes=[
+                half(6 * CH, C),
                 small(), small(), small(), small(),
                 table(), table(), table(), table(),
                 half(LO * CH, POINTS),
@@ -547,16 +622,15 @@
                 half(C, PATCH), half(C, PATCH), half(C, PATCH), half(C, PATCH), half(C, PATCH),
                 half(PATCH, C), half(2, C, PATCH), half(2, 2 * HD, PATCH),
                 full(2, PATCH, COLS), full(2, 8, COLS), half(2, PATCH, COLS),
-                half(BANDS, CH, PATCH), half(BANDS, CH, PATCH),
-                full(2, PATCH), full(BANDS, 2, PATCH),
+                half(BANDS, CH, PATCH), full(2, PATCH), full(BANDS, 2, PATCH),
                 half(GROUPS, PROWS, LO * CH), half(GROUPS, PROWS, LO * CH),
                 full(CHI, LO * CH), full(CHI, LO * CH),
-                full(BANDS, CH, CHI), full(BANDS, CH, CHI),
-                half(BANDS, CH2, CHI), half(BANDS, CH2, CHI),
-                half(LO * CH2, 8 * PROWS),
-                half(GROUPS, PROWS, LO * CH2), half(GROUPS, PROWS, LO * CH2),
+                half(BANDS, CH, CHI), half(BANDS, CH, CHI), half(BANDS, CH2, CHI),
+                half(LO * CH, 8 * PROWS),
+                half(GROUPS, PROWS, LO * CH), half(GROUPS, PROWS, LO * CH),
+                half(BANDS, CH, PATCH), half(BANDS, CH, PATCH), half(BANDS, CH2, PATCH),
                 pltpu.SemaphoreType.DMA((5, GROUPS)), pltpu.SemaphoreType.DMA((5, GROUPS)),
-                pltpu.SemaphoreType.DMA((6, BANDS)), pltpu.SemaphoreType.DMA((6, BANDS)),
+                pltpu.SemaphoreType.DMA((8, BANDS)), pltpu.SemaphoreType.DMA((8, BANDS)),
             ],
             compiler_params=pltpu.CompilerParams(
                 collective_id=0, has_side_effects=True, vmem_limit_bytes=56 * 1024 * 1024
@@ -565,10 +639,12 @@
             feats,
             hilbert_pos.reshape(1, POINTS),
             cell_of.reshape(1, POINTS),
-            own,
+            w_qkv.transpose(0, 2, 1).reshape(-1, C),
+            w_proj,
+            w_pool.T,
             ln_attn.reshape(1, C),
             ln_pool.reshape(1, C),
-        )
+        ))
     )
 
 

time: 176 us -> 173 us (0.983)
    unnamed x5 -> x6, local copies, waits for them, and re-layouts: 4.6 us -> 3.21 us
    pallas_call x1 -> x2, Pallas kernels: 169 us -> 168 us  [the longest x1 167 us: on_device(): pl.pallas_call(kernel, out_shape=[jax.ShapeDtypeStruct((BANDS, CH, PATCH)...]
where the time goes in v3:
time: 173 us; the launch traced here: 172 us
  Pallas kernels  168 us (97%)
  local copies, waits for them, and re-layouts  3.21 us (2%)
    pallas_call x1, Pallas kernels, on_device(): pl.pallas_call(kernel, out_shape=[jax.ShapeDtypeStruct((BANDS, CH, PATCH)...  167 us

profile of v3, /device:TPU:1, one launch (start us, length us, event | category | flops | bytes accessed | tf_op | source)
XLA Modules:
  0.0 171.8 jit_solution(16823146045052854934)
XLA Ops:
  0.6 166.6 %shard_map.103 = (bf16[8,32,1024]{2,1,0:T(8,128)(2,1)}, bf16[8,64,256]{2,1,0:T(8,128)(2,1)}, bf16[8,64,1024]{2,1,0:T(8,128)(2,1)}) custom-call(bf16[32,8192]{1,0:T(8,128)(2,1)} %feats_ref.1, s32[1,8192]{1,0:T(1,128)} %bitcast.9, s32[1,8192]{1,0:T(1,128)} %bitcast.10, bf16[96,256]{1,0:T(8,128)(2,1)} %bitcast.8, bf16[32,256]{1,0:T(8,128)(2,1)} %proj_ref.1, ...), custom_call_target="tpu_custom_call" | custom-call | tf_op jit(solution)/shard_map/pallas_call | solution.py:604
  167.2 0.0 copy-start
  167.2 1.2 copy-done
  168.5 0.0 copy-start.1
  168.5 1.0 copy-done.1
  169.5 0.0 copy-start.2
  169.5 0.9 copy-done.2
  170.4 1.3 shard_map.104
Async XLA Ops:
  167.2 1.2 copy-start
  168.5 1.0 copy-start.1
  169.5 0.9 copy-start.2

commit v4 on v3

--- a/solution.py
+++ b/solution.py
@@ -71,16 +71,17 @@
     k = 512
     before = lax.broadcasted_iota(jnp.int32, (k, k), 0) < lax.broadcasted_iota(jnp.int32, (k, k), 1)
     before = jnp.where(before, 1.0, 0.0).astype(BF)
+    goals = [slot_of(goal_ref[:, j * k : (j + 1) * k] >> bits) for j in range(POINTS // k)]
+    hot = jnp.concatenate([one_hot(goal, 0, GROUPS) for goal in goals], axis=0)
+    running = jnp.dot(hot, before, preferred_element_type=F32)
     carry = jnp.zeros((GROUPS, 1), F32)
-    for j in range(POINTS // k):
+    for j, goal in enumerate(goals):
         at = slice(j * k % PATCH, j * k % PATCH + k)
         of = slice(j * k // PATCH, j * k // PATCH + 1)
-        goal = slot_of(goal_ref[:, j * k : (j + 1) * k] >> bits)
         member = lax.broadcasted_iota(jnp.int32, (GROUPS, k), 0) == goal
-        hot = jnp.where(member, 1.0, 0.0)
-        running = jnp.dot(hot.astype(BF), before, preferred_element_type=F32) + carry
-        carry = carry + jnp.sum(hot, axis=1, keepdims=True)
-        rank = jnp.sum(hot * running, axis=0, keepdims=True).astype(jnp.int32)
+        ranks = running[j * GROUPS : (j + 1) * GROUPS]
+        rank = jnp.sum(jnp.where(member, ranks + carry, 0.0), axis=0, keepdims=True).astype(jnp.int32)
+        carry = carry + ranks[:, k - 1 :] + jnp.where(member[:, k - 1 :], 1.0, 0.0)
         low = jnp.zeros_like(rank)
         for l in range(1, LO):
             low += jnp.where(rank >= l * rows, 1, 0)
@@ -90,26 +91,25 @@
 
 def make_table(rows, bits, value_ref, row_ref, low_ref, table_ref):
     k = 512
-    table = jnp.zeros((GROUPS * LO, 2 * TAB), F32)
+    table = jnp.zeros((GROUPS * 4, 2 * TAB), F32)
     for j in range(POINTS // k):
         at = slice(j * k % PATCH, j * k % PATCH + k)
         of = slice(j * k // PATCH, j * k // PATCH + 1)
         values = value_ref[:, j * k : (j + 1) * k]
-        goal = slot_of(values >> bits)
+        goal, low = slot_of(values >> bits), low_ref[of, at]
         value = (values & ((1 << bits) - 1)) + 1
-        which = lax.broadcasted_iota(jnp.int32, (TAB, k), 0) == row_ref[of, at] - goal * rows
+        lane = row_ref[of, at] - goal * rows + (low & 1) * (TAB // 2)
+        which = lax.broadcasted_iota(jnp.int32, (TAB, k), 0) == lane
         parts = [
             jnp.where(which, part.astype(F32), 0.0) for part in (value >> 7, value & 127)
         ]
         marks = jnp.concatenate(parts, axis=0).astype(BF)
         table += lax.dot_general(
-            one_hot(goal * LO + low_ref[of, at], 0, GROUPS * LO),
-            marks,
-            NT,
-            preferred_element_type=F32,
+            one_hot(goal * 4 + (low >> 1), 0, GROUPS * 4), marks, NT, preferred_element_type=F32
         )
     table = (table[:, :TAB] * 128.0 + table[:, TAB:]).astype(jnp.int32) - 1
-    table_ref[...] = table.reshape(GROUPS, LO, TAB)
+    for t in range(GROUPS):
+        table_ref[t] = table[t * 4 : (t + 1) * 4]
 
 
 def place(row_ref, spread_ref, first, count):
@@ -288,7 +288,11 @@
 
 
 def lanes_of(table_ref, group, rows):
-    return jnp.concatenate([table_ref[group * 8 + i, :, :rows] for i in range(8)], axis=1)
+    halves = [
+        jnp.concatenate([table_ref[group * 8 + i][:, at : at + rows] for i in range(8)], axis=1)
+        for at in (0, TAB // 2)
+    ]
+    return [halves[l % 2][l // 2 : l // 2 + 1] for l in range(LO)]
 
 
 def kernel(
@@ -381,7 +385,6 @@
     gather.start()
     rank_points(PROWS, 11, cell_ref, p_row_ref, p_low_ref)
     make_table(PROWS, 11, cell_ref, p_row_ref, p_low_ref, cell_out)
-    lax.fori_loop(0, 4, lambda i, _: cells.start(i) or 0, 0)
 
     def first_group(g, _):
         landings.wait(g)
@@ -391,14 +394,14 @@
         landing = lanes_of(land_in, g, HROWS)
         for l in range(LO):
             spread_ref[:, l * k : (l + 1) * k] = spread(
-                turned[l * CH : (l + 1) * CH], (landing[l : l + 1] >> 7) & 7
+                turned[l * CH : (l + 1) * CH], (landing[l] >> 7) & 7
             )
-        rows = (landing >> 10) * 128 + (landing & 127)
+        rows = [(each >> 10) * 128 + (each & 127) for each in landing]
         for m in range(2):
             total = jnp.zeros((512, LO * CH), F32)
             for l in range(LO):
                 total += lax.dot_general(
-                    one_hot(rows[l : l + 1], m * 512, 512),
+                    one_hot(rows[l], m * 512, 512),
                     spread_ref[:, l * k : (l + 1) * k],
                     NT,
                     preferred_element_type=F32,
@@ -415,6 +418,7 @@
         return 0
 
     lax.fori_loop(0, 4, first_group, 0)
+    lax.fori_loop(0, 4, lambda i, _: cells.start(i) or 0, 0)
     gather.wait()
     patches.wait()
 
@@ -477,8 +481,8 @@
         ones = jnp.ones((CH, k), F32)
         for l in range(LO):
             count_ref[...] += lax.dot_general(
-                one_hot(cell[l : l + 1] & (CHI - 1), 0, CHI),
-                spread(ones, cell[l : l + 1] >> 8),
+                one_hot(cell[l] & (CHI - 1), 0, CHI),
+                spread(ones, cell[l] >> 8),
                 NT,
                 preferred_element_type=F32,
             )
@@ -492,8 +496,8 @@
         cell = lanes_of(cell_in, g, PROWS)
         for l in range(LO):
             sum_ref[...] += lax.dot_general(
-                one_hot(cell[l : l + 1] & (CHI - 1), 0, CHI),
-                spread(turned[l * CH : (l + 1) * CH], cell[l : l + 1] >> 8),
+                one_hot(cell[l] & (CHI - 1), 0, CHI),
+                spread(turned[l * CH : (l + 1) * CH], cell[l] >> 8),
                 NT,
                 preferred_element_type=F32,
             )
@@ -508,10 +512,10 @@
         means_of = mean_ref[...].reshape(C, CHI)
         for l in range(LO):
             product = jnp.dot(
-                means_of, one_hot(cell[l : l + 1] & (CHI - 1), 0, CHI), preferred_element_type=F32
+                means_of, one_hot(cell[l] & (CHI - 1), 0, CHI), preferred_element_type=F32
             )
             turned_ref[l * CH : (l + 1) * CH, :] = gather_low(
-                product, cell[l : l + 1] >> 8, CH
+                product, cell[l] >> 8, CH
             ).astype(BF)
         back_out[pl.ds(g * 8, 8)] = turned_ref[...].T.reshape(8, PROWS, LO * CH)
         back.start(g)
@@ -586,7 +590,7 @@
 
 def on_device(feats, hilbert_pos, ln_attn, w_qkv, w_proj, ln_pool, w_pool, cell_of):
     small = lambda: pltpu.VMEM((BANDS, PATCH), jnp.int32)
-    table = lambda: pltpu.VMEM((GROUPS, LO, TAB), jnp.int32)
+    table = lambda: pltpu.VMEM((GROUPS, 4, TAB), jnp.int32)
     half = lambda *dims: pltpu.VMEM(dims, BF)
     full = lambda *dims: pltpu.VMEM(dims, F32)
     settle = pl.pallas_call(
@@ -598,7 +602,7 @@
         ],
         in_specs=[INSIDE] * 3,
         out_specs=[INSIDE] * 3,
-        compiler_params=pltpu.CompilerParams(vmem_limit_bytes=16 * 1024 * 1024),
+        compiler_params=pltpu.CompilerParams(vmem_limit_bytes=60 * 1024 * 1024),
     )
     return tuple(
         settle(*pl.pallas_call(

time: 173 us -> 169 us (0.977)
  local copies, waits for them, and re-layouts: 3.21 us -> 0 us
    unnamed x6 -> x0, local copies, waits for them, and re-layouts: 3.21 us -> none
where the time goes in v4:
time: 169 us
  Pallas kernels  168 us (99%)
    pallas_call x1, Pallas kernels, on_device(): pl.pallas_call(kernel, out_shape=[jax.ShapeDtypeStruct((BANDS, CH, PATCH)...  165 us

profile of v4, /device:TPU:1, one launch (start us, length us, event | category | flops | bytes accessed | tf_op | source)
XLA Modules:
  0.0 168.8 jit_solution(10937571495829146979)
XLA Ops:
  0.6 165.4 %shard_map.103 = (bf16[8,32,1024]{2,1,0:T(8,128)(2,1)}, bf16[8,64,256]{2,1,0:T(8,128)(2,1)}, bf16[8,64,1024]{2,1,0:T(8,128)(2,1)}) custom-call(bf16[32,8192]{1,0:T(8,128)(2,1)} %feats_ref.1, s32[1,8192]{1,0:T(1,128)} %bitcast.9, s32[1,8192]{1,0:T(1,128)} %bitcast.10, bf16[96,256]{1,0:T(8,128)(2,1)} %bitcast.8, bf16[32,256]{1,0:T(8,128)(2,1)} %proj_ref.1, ...), custom_call_target="tpu_custom_call" | custom-call | tf_op jit(solution)/shard_map/pallas_call | solution.py:608
  166.0 2.7 %shard_map.104 = (bf16[32,8192]{1,0:T(8,128)(2,1)}, bf16[64,2048]{1,0:T(8,128)(2,1)}, bf16[64,8192]{1,0:T(8,128)(2,1)}) custom-call(bf16[8,32,1024]{2,1,0:T(8,128)(2,1)} %get-tuple-element.6.block_in, bf16[8,64,256]{2,1,0:T(8,128)(2,1)} %get-tuple-element.7.table_in, bf16[8,64,1024]{2,1,0:T(8,128)(2,1)} %get-tuple-element.8.result_in), custom_call_target="tpu_custom_call" | custom-call | tf_op jit(solution)/shard_map/pallas_call | solution.py:608

commit v5 on v4

--- a/solution.py
+++ b/solution.py
@@ -19,6 +19,8 @@
 LO = 8
 TAB = 128
 OWN = 1
+SET = 4
+SETS = GROUPS // SET
 INSIDE = pl.BlockSpec(memory_space=pltpu.VMEM)
 COLS = 512
 HROWS = 64
@@ -172,14 +174,14 @@
         lax.fori_loop(0, count, one, 0)
 
     def start(self, group):
-        self.each(group * 8, 8, lambda copy: copy.start())
-
-        @pl.when(group == OWN // 8)
+        self.each(group * SET, SET, lambda copy: copy.start())
+
+        @pl.when(group == OWN // SET)
         def _():
             self.dst[OWN] = self.src[OWN]
 
     def wait(self, group):
-        self.each(group * 8, 8, lambda copy: copy.wait_recv())
+        self.each(group * SET, SET, lambda copy: copy.wait_recv())
 
     def finish(self):
         self.each(0, GROUPS, lambda copy: copy.wait_send())
@@ -289,7 +291,7 @@
 
 def lanes_of(table_ref, group, rows):
     halves = [
-        jnp.concatenate([table_ref[group * 8 + i][:, at : at + rows] for i in range(8)], axis=1)
+        jnp.concatenate([table_ref[group * SET + i][:, at : at + rows] for i in range(SET)], axis=1)
         for at in (0, TAB // 2)
     ]
     return [halves[l % 2][l // 2 : l // 2 + 1] for l in range(LO)]
@@ -327,8 +329,8 @@
     patches = narrow(1, patch_out, patch_in)
     blocks = narrow(2, block_out, block_in)
     stats = narrow(5, stat_out, stat_in, True)
-    points = narrow(6, point_out, point_in)
-    results = narrow(7, result_out, result_in)
+    points = [narrow(6 + i, point_out.at[i], point_in.at[i]) for i in range(2)]
+    results = [narrow(8 + i, result_out.at[i], result_in.at[i]) for i in range(2)]
     means = narrow(3, mean_ref, mean_in)
     tables = narrow(4, table_out, table_in)
 
@@ -365,8 +367,9 @@
         spread_ref[:, at] = spread(feats_ref[:, at], low_ref[j : j + 1, :])
 
     def first_block(g, _):
-        chunk = place(row_ref, spread_ref, g * 512, 512).astype(BF)
-        first_out[pl.ds(g * 8, 8)] = chunk.reshape(8, HROWS, LO * CH)
+        count = SET * HROWS
+        chunk = place(row_ref, spread_ref, g * count, count).astype(BF)
+        first_out[pl.ds(g * SET, SET)] = chunk.reshape(SET, HROWS, LO * CH)
 
         @pl.when(g == 0)
         def _():
@@ -374,14 +377,14 @@
 
         first.start(g)
 
-        @pl.when(g == 0)
+        @pl.when(g == 1)
         def _():
             make_table(HROWS, 13, hilbert_ref, row_ref, low_ref, land_out)
-            lax.fori_loop(0, 4, lambda i, _: landings.start(i) or 0, 0)
-
-        return 0
-
-    lax.fori_loop(0, 4, first_block, 0)
+            lax.fori_loop(0, SETS, lambda i, _: landings.start(i) or 0, 0)
+
+        return 0
+
+    lax.fori_loop(0, SETS, first_block, 0)
     gather.start()
     rank_points(PROWS, 11, cell_ref, p_row_ref, p_low_ref)
     make_table(PROWS, 11, cell_ref, p_row_ref, p_low_ref, cell_out)
@@ -389,8 +392,8 @@
     def first_group(g, _):
         landings.wait(g)
         first.wait(g)
-        k = 8 * HROWS
-        turned = first_in[pl.ds(g * 8, 8)].reshape(k, LO * CH).T
+        k = SET * HROWS
+        turned = first_in[pl.ds(g * SET, SET)].reshape(k, LO * CH).T
         landing = lanes_of(land_in, g, HROWS)
         for l in range(LO):
             spread_ref[:, l * k : (l + 1) * k] = spread(
@@ -410,15 +413,15 @@
             total = jnp.where(g == 0, total, total + acc_ref[at, :])
             acc_ref[at, :] = total
 
-            @pl.when(g == 3)
+            @pl.when(g == SETS - 1)
             def _():
                 patch_out[m * 4 : (m + 1) * 4] = total.astype(BF).reshape(4, PATCH // LO, LO * CH)
                 patches.start_half(m)
 
         return 0
 
-    lax.fori_loop(0, 4, first_group, 0)
-    lax.fori_loop(0, 4, lambda i, _: cells.start(i) or 0, 0)
+    lax.fori_loop(0, SETS, first_group, 0)
+    lax.fori_loop(0, SETS, lambda i, _: cells.start(i) or 0, 0)
     gather.wait()
     patches.wait()
 
@@ -453,6 +456,7 @@
     stats.wait()
     blocks.wait()
 
+    k = SET * PROWS
     gains2 = jnp.broadcast_to(gain2_ref[...], (8, C)).T[:, :1].reshape(BANDS, CH, 1)
     gain2 = jnp.zeros((CH, 1), F32)
     for n in range(BANDS):
@@ -465,15 +469,14 @@
         spread_ref[:, at] = spread(pooled, p_low_ref[j : j + 1, :])
 
     def second_block(g, _):
-        chunk = place(p_row_ref, spread_ref, g * 384, 384).astype(BF)
-        second_out[pl.ds(g * 8, 8)] = chunk.reshape(8, PROWS, LO * CH)
+        chunk = place(p_row_ref, spread_ref, g * k, k).astype(BF)
+        second_out[pl.ds(g * SET, SET)] = chunk.reshape(SET, PROWS, LO * CH)
         second.start(g)
         return 0
 
-    lax.fori_loop(0, 4, second_block, 0)
+    lax.fori_loop(0, SETS, second_block, 0)
     sum_ref[...] = jnp.zeros_like(sum_ref)
     count_ref[...] = jnp.zeros_like(count_ref)
-    k = 8 * PROWS
 
     def count_group(g, _):
         cells.wait(g)
@@ -488,11 +491,11 @@
             )
         return 0
 
-    lax.fori_loop(0, 4, count_group, 0)
+    lax.fori_loop(0, SETS, count_group, 0)
 
     def second_group(g, _):
         second.wait(g)
-        turned = second_in[pl.ds(g * 8, 8)].reshape(k, LO * CH).T
+        turned = second_in[pl.ds(g * SET, SET)].reshape(k, LO * CH).T
         cell = lanes_of(cell_in, g, PROWS)
         for l in range(LO):
             sum_ref[...] += lax.dot_general(
@@ -503,7 +506,7 @@
             )
         return 0
 
-    lax.fori_loop(0, 4, second_group, 0)
+    lax.fori_loop(0, SETS, second_group, 0)
     mean = (sum_ref[...] / jnp.maximum(count_ref[...], 1.0)).T.astype(BF)
     mean_ref[...] = mean.reshape(BANDS, CH, CHI)
 
@@ -517,11 +520,11 @@
             turned_ref[l * CH : (l + 1) * CH, :] = gather_low(
                 product, cell[l] >> 8, CH
             ).astype(BF)
-        back_out[pl.ds(g * 8, 8)] = turned_ref[...].T.reshape(8, PROWS, LO * CH)
+        back_out[pl.ds(g * SET, SET)] = turned_ref[...].T.reshape(SET, PROWS, LO * CH)
         back.start(g)
         return 0
 
-    lax.fori_loop(0, 4, give_group, 0)
+    lax.fori_loop(0, SETS, give_group, 0)
     means.start()
     means.wait()
 
@@ -533,51 +536,55 @@
 
     def take_group(g, _):
         back.wait(g)
-        turned_ref[...] = back_in[pl.ds(g * 8, 8)].reshape(k, LO * CH).T
-        for half_of in range(2):
-            for j in range(half_of * 4, half_of * 4 + 4):
+        turned_ref[...] = back_in[pl.ds(g * SET, SET)].reshape(k, LO * CH).T
+        for part in range(2):
+            columns = slice(part * COLS, (part + 1) * COLS)
+            for j in range(BANDS):
                 product = jnp.dot(
                     turned_ref[...],
-                    one_hot(p_row_ref[j : j + 1, :], g * k, k),
+                    one_hot(p_row_ref[j : j + 1, columns], g * k, k),
                     preferred_element_type=F32,
                 )
-                part = gather_low(product, p_low_ref[j : j + 1, :], CH)
-                before = jnp.where(g == 0, 0.0, point_out[j].astype(F32))
-                point_out[j] = (before + part).astype(BF)
-
-            @pl.when(g == 3)
+                taken = gather_low(product, p_low_ref[j : j + 1, columns], CH)
+                before = jnp.where(g == 0, 0.0, point_out[part, j].astype(F32))
+                point_out[part, j] = (before + taken).astype(BF)
+
+            @pl.when(g == SETS - 1)
             def _():
-                points.start_half(half_of)
+                points[part].start()
 
         return 0
 
     point_out[...] = jnp.zeros_like(point_out)
-    lax.fori_loop(0, 4, take_group, 0)
-    points.wait()
-
-    def project_for(step, _):
-        n = (mine + step) % BANDS
-        result_out[n] = gelu(
-            jnp.dot(
-                weights_ref[n, 4 * CH :, :],
-                point_in[...].reshape(C, PATCH),
-                preferred_element_type=F32,
+    lax.fori_loop(0, SETS, take_group, 0)
+
+    for part in range(2):
+        points[part].wait()
+
+        def project_for(step, _):
+            n = (mine + step) % BANDS
+            result_out[part, n] = gelu(
+                jnp.dot(
+                    weights_ref[n, 4 * CH :, :],
+                    point_in[part].reshape(C, COLS),
+                    preferred_element_type=F32,
+                )
             )
-        )
-
-        @pl.when(step != BANDS)
-        def _():
-            results.copy(step).start()
-
-        return 0
-
-    lax.fori_loop(1, BANDS + 1, project_for, 0)
-    result_in[mine] = result_out[mine]
-    results.wait()
+
+            @pl.when(step != BANDS)
+            def _():
+                results[part].copy(step).start()
+
+            return 0
+
+        lax.fori_loop(1, BANDS + 1, project_for, 0)
+        result_in[part, mine] = result_out[part, mine]
+    for part in range(2):
+        results[part].wait()
     tables.wait()
     for each in (landings, first, cells, second, back):
         each.finish()
-    for each in (gather, patches, blocks, stats, means, tables, points, results):
+    for each in (gather, patches, blocks, stats, means, tables, *points, *results):
         each.finish()
 
 
@@ -585,7 +592,9 @@
     for n in range(BANDS):
         block_ref[:, n * PATCH : (n + 1) * PATCH] = block_in[n]
         coarse_ref[:, n * CHI : (n + 1) * CHI] = table_in[n]
-        unpooled_ref[:, n * PATCH : (n + 1) * PATCH] = result_in[n]
+        for part in range(2):
+            at = slice(n * PATCH + part * COLS, n * PATCH + (part + 1) * COLS)
+            unpooled_ref[:, at] = result_in[part, n]
 
 
 def on_device(feats, hilbert_pos, ln_attn, w_qkv, w_proj, ln_pool, w_pool, cell_of):
@@ -610,7 +619,7 @@
             out_shape=[
                 jax.ShapeDtypeStruct((BANDS, CH, PATCH), BF),
                 jax.ShapeDtypeStruct((BANDS, CH2, CHI), BF),
-                jax.ShapeDtypeStruct((BANDS, CH2, PATCH), BF),
+                jax.ShapeDtypeStruct((2, BANDS, CH2, COLS), BF),
             ],
             in_specs=[INSIDE] * 8,
             out_specs=[INSIDE] * 3,
@@ -630,11 +639,11 @@
                 half(GROUPS, PROWS, LO * CH), half(GROUPS, PROWS, LO * CH),
                 full(CHI, LO * CH), full(CHI, LO * CH),
                 half(BANDS, CH, CHI), half(BANDS, CH, CHI), half(BANDS, CH2, CHI),
-                half(LO * CH, 8 * PROWS),
+                half(LO * CH, SET * PROWS),
                 half(GROUPS, PROWS, LO * CH), half(GROUPS, PROWS, LO * CH),
-                half(BANDS, CH, PATCH), half(BANDS, CH, PATCH), half(BANDS, CH2, PATCH),
+                half(2, BANDS, CH, COLS), half(2, BANDS, CH, COLS), half(2, BANDS, CH2, COLS),
                 pltpu.SemaphoreType.DMA((5, GROUPS)), pltpu.SemaphoreType.DMA((5, GROUPS)),
-                pltpu.SemaphoreType.DMA((8, BANDS)), pltpu.SemaphoreType.DMA((8, BANDS)),
+                pltpu.SemaphoreType.DMA((10, BANDS)), pltpu.SemaphoreType.DMA((10, BANDS)),
             ],
             compiler_params=pltpu.CompilerParams(
                 collective_id=0, has_side_effects=True, vmem_limit_bytes=56 * 1024 * 1024

time: 169 us -> 169 us (level)
  no operation moved by 1% of the time
where the time goes in v5:
time: 169 us
  Pallas kernels  169 us (100%)
    pallas_call x1, Pallas kernels, on_device(): pl.pallas_call(kernel, out_shape=[jax.ShapeDtypeStruct((BANDS, CH, PATCH)...  166 us

profile of v5, /device:TPU:1, one launch (start us, length us, event | category | flops | bytes accessed | tf_op | source)
XLA Modules:
  0.0 169.3 jit_solution(4458297638587366149)
XLA Ops:
  0.6 166.0 %shard_map.103 = (bf16[8,32,1024]{2,1,0:T(8,128)(2,1)}, bf16[8,64,256]{2,1,0:T(8,128)(2,1)}, bf16[2,8,64,512]{3,2,1,0:T(8,128)(2,1)}) custom-call(bf16[32,8192]{1,0:T(8,128)(2,1)} %feats_ref.1, s32[1,8192]{1,0:T(1,128)} %bitcast.9, s32[1,8192]{1,0:T(1,128)} %bitcast.10, bf16[96,256]{1,0:T(8,128)(2,1)} %bitcast.8, bf16[32,256]{1,0:T(8,128)(2,1)} %proj_ref.1, ...), custom_call_target="tpu_custom_call" | custom-call | tf_op jit(solution)/shard_map/pallas_call | solution.py:617
  166.6 2.7 %shard_map.104 = (bf16[32,8192]{1,0:T(8,128)(2,1)}, bf16[64,2048]{1,0:T(8,128)(2,1)}, bf16[64,8192]{1,0:T(8,128)(2,1)}) custom-call(bf16[8,32,1024]{2,1,0:T(8,128)(2,1)} %get-tuple-element.6.block_in, bf16[8,64,256]{2,1,0:T(8,128)(2,1)} %get-tuple-element.7.table_in, bf16[2,8,64,512]{3,2,1,0:T(8,128)(2,1)} %get-tuple-element.8.result_in), custom_call_target="tpu_custom_call" | custom-call | tf_op jit(solution)/shard_map/pallas_call | solution.py:617

commit v6 on v5

--- a/solution.py
+++ b/solution.py
@@ -21,6 +21,8 @@
 OWN = 1
 SET = 4
 SETS = GROUPS // SET
+POOL_SET = 8
+POOL_SETS = GROUPS // POOL_SET
 INSIDE = pl.BlockSpec(memory_space=pltpu.VMEM)
 COLS = 512
 HROWS = 64
@@ -149,8 +151,9 @@
 
 
 class Wide:
-    def __init__(self, src, dst, send_sem, recv_sem, sign):
+    def __init__(self, size, src, dst, send_sem, recv_sem, sign):
         self.src, self.dst, self.send_sem, self.recv_sem, self.sign = src, dst, send_sem, recv_sem, sign
+        self.size = size
 
     def each(self, first, count, act):
         def one(i, _):
@@ -174,14 +177,14 @@
         lax.fori_loop(0, count, one, 0)
 
     def start(self, group):
-        self.each(group * SET, SET, lambda copy: copy.start())
-
-        @pl.when(group == OWN // SET)
+        self.each(group * self.size, self.size, lambda copy: copy.start())
+
+        @pl.when(group == 0)
         def _():
             self.dst[OWN] = self.src[OWN]
 
     def wait(self, group):
-        self.each(group * SET, SET, lambda copy: copy.wait_recv())
+        self.each(group * self.size, self.size, lambda copy: copy.wait_recv())
 
     def finish(self):
         self.each(0, GROUPS, lambda copy: copy.wait_send())
@@ -289,9 +292,9 @@
     return (value * (1.0 + lax.erf(value * (0.5**0.5))) * 0.5).astype(BF)
 
 
-def lanes_of(table_ref, group, rows):
+def lanes_of(table_ref, group, size, rows):
     halves = [
-        jnp.concatenate([table_ref[group * SET + i][:, at : at + rows] for i in range(SET)], axis=1)
+        jnp.concatenate([table_ref[group * size + i][:, at : at + rows] for i in range(size)], axis=1)
         for at in (0, TAB // 2)
     ]
     return [halves[l % 2][l // 2 : l // 2 + 1] for l in range(LO)]
@@ -314,17 +317,17 @@
     me = lax.axis_index("wide")
     mine = lax.axis_index("narrow")
 
-    def wide(number, src, dst, sign=1):
-        return Wide(src, dst, wide_send.at[number], wide_recv.at[number], sign)
+    def wide(number, size, src, dst, sign=1):
+        return Wide(size, src, dst, wide_send.at[number], wide_recv.at[number], sign)
 
     def narrow(number, src, dst, whole=False):
         return Narrow(src, dst, narrow_send.at[number], narrow_recv.at[number], whole)
 
-    landings = wide(0, land_out, land_in)
-    first = wide(1, first_out, first_in)
-    cells = wide(2, cell_out, cell_in)
-    second = wide(3, second_out, second_in)
-    back = wide(4, back_out, back_in, -1)
+    landings = wide(0, SET, land_out, land_in)
+    first = wide(1, SET, first_out, first_in)
+    cells = wide(2, POOL_SET, cell_out, cell_in)
+    second = wide(3, POOL_SET, second_out, second_in)
+    back = wide(4, POOL_SET, back_out, back_in, -1)
     gather = narrow(0, own_ref, weights_ref, True)
     patches = narrow(1, patch_out, patch_in)
     blocks = narrow(2, block_out, block_in)
@@ -394,7 +397,7 @@
         first.wait(g)
         k = SET * HROWS
         turned = first_in[pl.ds(g * SET, SET)].reshape(k, LO * CH).T
-        landing = lanes_of(land_in, g, HROWS)
+        landing = lanes_of(land_in, g, SET, HROWS)
         for l in range(LO):
             spread_ref[:, l * k : (l + 1) * k] = spread(
                 turned[l * CH : (l + 1) * CH], (landing[l] >> 7) & 7
@@ -421,7 +424,7 @@
         return 0
 
     lax.fori_loop(0, SETS, first_group, 0)
-    lax.fori_loop(0, SETS, lambda i, _: cells.start(i) or 0, 0)
+    lax.fori_loop(0, POOL_SETS, lambda i, _: cells.start(i) or 0, 0)
     gather.wait()
     patches.wait()
 
@@ -456,7 +459,7 @@
     stats.wait()
     blocks.wait()
 
-    k = SET * PROWS
+    k = POOL_SET * PROWS
     gains2 = jnp.broadcast_to(gain2_ref[...], (8, C)).T[:, :1].reshape(BANDS, CH, 1)
     gain2 = jnp.zeros((CH, 1), F32)
     for n in range(BANDS):
@@ -470,17 +473,17 @@
 
     def second_block(g, _):
         chunk = place(p_row_ref, spread_ref, g * k, k).astype(BF)
-        second_out[pl.ds(g * SET, SET)] = chunk.reshape(SET, PROWS, LO * CH)
+        second_out[pl.ds(g * POOL_SET, POOL_SET)] = chunk.reshape(POOL_SET, PROWS, LO * CH)
         second.start(g)
         return 0
 
-    lax.fori_loop(0, SETS, second_block, 0)
+    lax.fori_loop(0, POOL_SETS, second_block, 0)
     sum_ref[...] = jnp.zeros_like(sum_ref)
     count_ref[...] = jnp.zeros_like(count_ref)
 
     def count_group(g, _):
         cells.wait(g)
-        cell = lanes_of(cell_in, g, PROWS)
+        cell = lanes_of(cell_in, g, POOL_SET, PROWS)
         ones = jnp.ones((CH, k), F32)
         for l in range(LO):
             count_ref[...] += lax.dot_general(
@@ -491,12 +494,12 @@
             )
         return 0
 
-    lax.fori_loop(0, SETS, count_group, 0)
+    lax.fori_loop(0, POOL_SETS, count_group, 0)
 
     def second_group(g, _):
         second.wait(g)
-        turned = second_in[pl.ds(g * SET, SET)].reshape(k, LO * CH).T
-        cell = lanes_of(cell_in, g, PROWS)
+        turned = second_in[pl.ds(g * POOL_SET, POOL_SET)].reshape(k, LO * CH).T
+        cell = lanes_of(cell_in, g, POOL_SET, PROWS)
         for l in range(LO):
             sum_ref[...] += lax.dot_general(
                 one_hot(cell[l] & (CHI - 1), 0, CHI),
@@ -506,12 +509,12 @@
             )
         return 0
 
-    lax.fori_loop(0, SETS, second_group, 0)
+    lax.fori_loop(0, POOL_SETS, second_group, 0)
     mean = (sum_ref[...] / jnp.maximum(count_ref[...], 1.0)).T.astype(BF)
     mean_ref[...] = mean.reshape(BANDS, CH, CHI)
 
     def give_group(g, _):
-        cell = lanes_of(cell_in, g, PROWS)
+        cell = lanes_of(cell_in, g, POOL_SET, PROWS)
         means_of = mean_ref[...].reshape(C, CHI)
         for l in range(LO):
             product = jnp.dot(
@@ -520,23 +523,16 @@
             turned_ref[l * CH : (l + 1) * CH, :] = gather_low(
                 product, cell[l] >> 8, CH
             ).astype(BF)
-        back_out[pl.ds(g * SET, SET)] = turned_ref[...].T.reshape(SET, PROWS, LO * CH)
+        back_out[pl.ds(g * POOL_SET, POOL_SET)] = turned_ref[...].T.reshape(POOL_SET, PROWS, LO * CH)
         back.start(g)
         return 0
 
-    lax.fori_loop(0, SETS, give_group, 0)
+    lax.fori_loop(0, POOL_SETS, give_group, 0)
     means.start()
-    means.wait()
-
-    for n in range(BANDS):
-        table_out[n] = gelu(
-            jnp.dot(weights_ref[n, 4 * CH :, :], mean_in[...].reshape(C, CHI), preferred_element_type=F32)
-        )
-    tables.start()
 
     def take_group(g, _):
         back.wait(g)
-        turned_ref[...] = back_in[pl.ds(g * SET, SET)].reshape(k, LO * CH).T
+        turned_ref[...] = back_in[pl.ds(g * POOL_SET, POOL_SET)].reshape(k, LO * CH).T
         for part in range(2):
             columns = slice(part * COLS, (part + 1) * COLS)
             for j in range(BANDS):
@@ -549,14 +545,21 @@
                 before = jnp.where(g == 0, 0.0, point_out[part, j].astype(F32))
                 point_out[part, j] = (before + taken).astype(BF)
 
-            @pl.when(g == SETS - 1)
+            @pl.when(g == POOL_SETS - 1)
             def _():
                 points[part].start()
 
         return 0
 
     point_out[...] = jnp.zeros_like(point_out)
-    lax.fori_loop(0, SETS, take_group, 0)
+    lax.fori_loop(0, POOL_SETS, take_group, 0)
+    means.wait()
+
+    for n in range(BANDS):
+        table_out[n] = gelu(
+            jnp.dot(weights_ref[n, 4 * CH :, :], mean_in[...].reshape(C, CHI), preferred_element_type=F32)
+        )
+    tables.start()
 
     for part in range(2):
         points[part].wait()
@@ -639,7 +642,7 @@
                 half(GROUPS, PROWS, LO * CH), half(GROUPS, PROWS, LO * CH),
                 full(CHI, LO * CH), full(CHI, LO * CH),
                 half(BANDS, CH, CHI), half(BANDS, CH, CHI), half(BANDS, CH2, CHI),
-                half(LO * CH, SET * PROWS),
+                half(LO * CH, POOL_SET * PROWS),
                 half(GROUPS, PROWS, LO * CH), half(GROUPS, PROWS, LO * CH),
                 half(2, BANDS, CH, COLS), half(2, BANDS, CH, COLS), half(2, BANDS, CH2, COLS),
                 pltpu.SemaphoreType.DMA((5, GROUPS)), pltpu.SemaphoreType.DMA((5, GROUPS)),

time: 169 us -> 170 us (level)
  no operation moved by 1% of the time
where the time goes in v6:
time: 170 us
  Pallas kernels  170 us (100%)
    pallas_call x1, Pallas kernels, on_device(): pl.pallas_call(kernel, out_shape=[jax.ShapeDtypeStruct((BANDS, CH, PATCH)...  167 us

profile of v6, /device:TPU:1, one launch (start us, length us, event | category | flops | bytes accessed | tf_op | source)
XLA Modules:
  0.0 170.3 jit_solution(2128950783972436540)
XLA Ops:
  0.6 166.9 %shard_map.103 = (bf16[8,32,1024]{2,1,0:T(8,128)(2,1)}, bf16[8,64,256]{2,1,0:T(8,128)(2,1)}, bf16[2,8,64,512]{3,2,1,0:T(8,128)(2,1)}) custom-call(bf16[32,8192]{1,0:T(8,128)(2,1)} %feats_ref.1, s32[1,8192]{1,0:T(1,128)} %bitcast.9, s32[1,8192]{1,0:T(1,128)} %bitcast.10, bf16[96,256]{1,0:T(8,128)(2,1)} %bitcast.8, bf16[32,256]{1,0:T(8,128)(2,1)} %proj_ref.1, ...), custom_call_target="tpu_custom_call" | custom-call | tf_op jit(solution)/shard_map/pallas_call | solution.py:620
  167.5 2.7 %shard_map.104 = (bf16[32,8192]{1,0:T(8,128)(2,1)}, bf16[64,2048]{1,0:T(8,128)(2,1)}, bf16[64,8192]{1,0:T(8,128)(2,1)}) custom-call(bf16[8,32,1024]{2,1,0:T(8,128)(2,1)} %get-tuple-element.6.block_in, bf16[8,64,256]{2,1,0:T(8,128)(2,1)} %get-tuple-element.7.table_in, bf16[2,8,64,512]{3,2,1,0:T(8,128)(2,1)} %get-tuple-element.8.result_in), custom_call_target="tpu_custom_call" | custom-call | tf_op jit(solution)/shard_map/pallas_call | solution.py:620

commit v7 on v4

--- a/solution.py
+++ b/solution.py
@@ -523,13 +523,6 @@
 
     lax.fori_loop(0, 4, give_group, 0)
     means.start()
-    means.wait()
-
-    for n in range(BANDS):
-        table_out[n] = gelu(
-            jnp.dot(weights_ref[n, 4 * CH :, :], mean_in[...].reshape(C, CHI), preferred_element_type=F32)
-        )
-    tables.start()
 
     def take_group(g, _):
         back.wait(g)
@@ -553,6 +546,13 @@
 
     point_out[...] = jnp.zeros_like(point_out)
     lax.fori_loop(0, 4, take_group, 0)
+    means.wait()
+
+    for n in range(BANDS):
+        table_out[n] = gelu(
+            jnp.dot(weights_ref[n, 4 * CH :, :], mean_in[...].reshape(C, CHI), preferred_element_type=F32)
+        )
+    tables.start()
     points.wait()
 
     def project_for(step, _):

time: 169 us -> 172 us (1.018)
  Pallas kernels: 168 us -> 170 us
    pallas_call x1, Pallas kernels: 165 us -> 168 us  [on_device(): pl.pallas_call(kernel, out_shape=[jax.ShapeDtypeStruct((BANDS, CH, PATCH)...]
where the time goes in v7:
time: 172 us; the launch traced here: 171 us
  Pallas kernels  170 us (99%)
    pallas_call x1, Pallas kernels, on_device(): pl.pallas_call(kernel, out_shape=[jax.ShapeDtypeStruct((BANDS, CH, PATCH)...  168 us

profile of v7, /device:TPU:1, one launch (start us, length us, event | category | flops | bytes accessed | tf_op | source)
XLA Modules:
  0.0 171.1 jit_solution(13086970070358550283)
XLA Ops:
  0.6 167.7 %shard_map.103 = (bf16[8,32,1024]{2,1,0:T(8,128)(2,1)}, bf16[8,64,256]{2,1,0:T(8,128)(2,1)}, bf16[8,64,1024]{2,1,0:T(8,128)(2,1)}) custom-call(bf16[32,8192]{1,0:T(8,128)(2,1)} %feats_ref.1, s32[1,8192]{1,0:T(1,128)} %bitcast.9, s32[1,8192]{1,0:T(1,128)} %bitcast.10, bf16[96,256]{1,0:T(8,128)(2,1)} %bitcast.8, bf16[32,256]{1,0:T(8,128)(2,1)} %proj_ref.1, ...), custom_call_target="tpu_custom_call" | custom-call | tf_op jit(solution)/shard_map/pallas_call | solution.py:608
  168.3 2.7 %shard_map.104 = (bf16[32,8192]{1,0:T(8,128)(2,1)}, bf16[64,2048]{1,0:T(8,128)(2,1)}, bf16[64,8192]{1,0:T(8,128)(2,1)}) custom-call(bf16[8,32,1024]{2,1,0:T(8,128)(2,1)} %get-tuple-element.6.block_in, bf16[8,64,256]{2,1,0:T(8,128)(2,1)} %get-tuple-element.7.table_in, bf16[8,64,1024]{2,1,0:T(8,128)(2,1)} %get-tuple-element.8.result_in), custom_call_target="tpu_custom_call" | custom-call | tf_op jit(solution)/shard_map/pallas_call | solution.py:608
